TPU v7x, 512 devices: a whole 4x4x16 slice. The times are simulated.
512 devices in a mesh: section: 64 (over z_lo, x, core), dp: 8 (over z_hi, y).
Axes of the slice: x: 4, y: 4, z: 16 (z_hi: 2, z_lo: 8; z = z_hi * 8 + z_lo), core: 2. Of those that a mesh axis runs over, the one named last changes fastest.
Arguments:
- inputs: bfloat16 [1024, 3072], P('dp'), may hold values from -6 to 6
- cotangent: bfloat16 [1024, 3072], P('dp'), may hold values from -6 to 6
- weight: bfloat16 [3072, 6144], P('dp', 'section'), may hold values from -6 to 6
- moment1: float32 [3072, 6144], P('dp', 'section'), may hold values from -2 to 2
- moment2: float32 [3072, 6144], P('dp', 'section'), may hold values from 0.05 to 1
Outputs:
- spare: bfloat16 [1024, 6144], P('dp', 'section')
- input_gradient: bfloat16 [1024, 6144], P('dp', 'section')
- new_weight: bfloat16 [3072, 6144], P('dp', 'section')
- new_moment1: float32 [3072, 6144], P('dp', 'section')
- new_moment2: float32 [3072, 6144], P('dp', 'section')
- new_copy: bfloat16 [3072, 6144], P('dp', 'section')
All inputs are finite; a program needn't handle non-finite values.
Results may differ from a plain program's by a relative error of at most 0.0058.
Values may be sent and summed in bfloat16 or wider, within the bound.
A program may use at most 64 MiB of HBM per device.

v0:
```python
import math

import jax
import jax.numpy as jnp
from jax import lax
from jax.sharding import PartitionSpec as P

D = 3072
SECTIONS = 2


NORM_EPS = 1e-05
FIRST_FIX = 0.6513215599
SECOND_FIX = 0.4012630607


def swapped(shard, axis, stride):
    return lax.ppermute(shard, axis, [(i, i ^ 1 << stride) for i in range(lax.axis_size(axis))])


def from_behind(shard, axis, by):
    peers = lax.axis_size(axis)
    pairs = [(i, i + by) for i in range(peers) if 0 <= i + by < peers]
    return lax.ppermute(shard, axis, pairs)


def gelu_value(z):
    return 0.5 * z * (1.0 + lax.erf(z * 0.7071067811865476))


def gelu_slope(z):
    return (
        0.5 * (1.0 + lax.erf(z * 0.7071067811865476))
        + z * jnp.exp(-0.5 * z * z) * 0.3989422804014327
    )


def layer_norm(rows):
    centre = jnp.mean(rows, axis=1, keepdims=True)
    centred = rows - centre
    variance = jnp.mean(centred * centred, axis=1, keepdims=True)
    inverse = lax.rsqrt(variance + NORM_EPS)
    return (centred * inverse, inverse)


def spread_lanes(piece, lanes):
    position = lax.axis_index("section")
    for level in range(lanes.bit_length() - 1):
        other = swapped(piece, "section", level)
        upper = position // 2**level % 2 == 1
        first = jnp.where(upper, other, piece)
        second = jnp.where(upper, piece, other)
        piece = jnp.concatenate([first, second], axis=1)
    return piece


def halve_lanes(full, lanes):
    position = lax.axis_index("section")
    for level in reversed(range(lanes.bit_length() - 1)):
        half = full.shape[1] // 2
        upper = position // 2**level % 2 == 1
        lower_part = full[:, :half]
        upper_part = full[:, half:]
        kept = jnp.where(upper, upper_part, lower_part)
        given = jnp.where(upper, lower_part, upper_part)
        full = kept + swapped(given, "section", level)
    return full


def lane_totals(stacked, lanes):
    for level in range(lanes.bit_length() - 1):
        stacked = stacked + swapped(stacked, "section", level)
    return stacked


def per_device(inputs, cotangent, weight, moment1, moment2):
    sections = SECTIONS
    lanes = lax.axis_size("section") // sections
    position = lax.axis_index("section")
    section_id = position // lanes
    lane = position % lanes
    width = weight.shape[1]
    tokens = inputs.shape[0]
    scale = 1.0 / math.sqrt(D)
    start_col = lane * width
    successor = from_behind(weight, "section", -lanes)
    own, follow = (
        lax.all_gather(weight, "dp", axis=0, tiled=True),
        lax.all_gather(successor, "dp", axis=0, tiled=True),
    )

    def advance(rows):
        normed, inverse = layer_norm(rows.astype(jnp.float32))
        mixed = (
            jnp.dot(normed.astype(jnp.bfloat16), own, preferred_element_type=jnp.float32) * scale
        )
        base = lax.dynamic_slice_in_dim(rows, start_col, width, 1).astype(jnp.float32)
        return ((base + gelu_value(mixed)).astype(jnp.bfloat16), mixed)

    def pause(rows):
        return (jnp.zeros((tokens, width), jnp.bfloat16), jnp.zeros((tokens, width), jnp.float32))

    current = inputs
    section_input = inputs
    own_out = jnp.zeros((tokens, width), jnp.bfloat16)
    own_mixed = jnp.zeros((tokens, width), jnp.float32)
    for step in range(sections):
        active = section_id == step
        produced, mixed = lax.cond(active, advance, pause, current)
        section_input = jnp.where(active, current, section_input)
        own_out = jnp.where(active, produced, own_out)
        own_mixed = jnp.where(active, mixed, own_mixed)
        if step + 1 < sections:
            current = spread_lanes(from_behind(produced, "section", lanes), lanes)
    whole = spread_lanes(own_out, lanes)
    normed_next, _ = layer_norm(whole.astype(jnp.float32))
    mixed_next = (
        jnp.dot(normed_next.astype(jnp.bfloat16), follow, preferred_element_type=jnp.float32)
        * scale
    )
    result = (own_out.astype(jnp.float32) + gelu_value(mixed_next)).astype(jnp.bfloat16)
    spare = jnp.where(section_id + 1 < sections, result, jnp.zeros_like(result))
    normed_all, inverse = layer_norm(section_input.astype(jnp.float32))
    lowered = normed_all.astype(jnp.bfloat16)
    normed_lane = lax.dynamic_slice_in_dim(normed_all, start_col, width, 1)
    upstream = lax.dynamic_slice_in_dim(cotangent, start_col, width, 1)
    slope_own = jnp.zeros((tokens, width), jnp.bfloat16)
    grad_own = jnp.zeros((tokens, width), jnp.bfloat16)

    def spread_back(slope):
        return (
            lax.dot_general(
                slope, own, (((1,), (1,)), ((), ())), preferred_element_type=jnp.float32
            )
            * scale
        )

    def still(slope):
        return jnp.zeros((tokens, D), jnp.float32)

    for step in reversed(range(sections)):
        active = section_id == step
        slope = (upstream.astype(jnp.float32) * gelu_slope(own_mixed)).astype(jnp.bfloat16)
        slope_own = jnp.where(active, slope, slope_own)
        partial_value = lax.cond(active, spread_back, still, slope)
        back = halve_lanes(partial_value, lanes)
        totals = lane_totals(
            jnp.stack([jnp.sum(back, axis=1), jnp.sum(back * normed_lane, axis=1)]), lanes
        )
        first = totals[0][:, None] / D
        second = totals[1][:, None] / D
        change = inverse * (back - first - normed_lane * second)
        renewed = (upstream.astype(jnp.float32) + change).astype(jnp.bfloat16)
        grad_own = jnp.where(active, renewed, grad_own)
        if step > 0:
            upstream = from_behind(renewed, "section", -lanes)
    gradient = lax.psum_scatter(
        (
            lax.dot_general(
                lowered, slope_own, (((0,), (0,)), ((), ())), preferred_element_type=jnp.float32
            )
            * scale
        ).astype(jnp.bfloat16),
        "dp",
        scatter_dimension=0,
        tiled=True,
    ).astype(jnp.float32)
    new_moment1 = 0.9 * moment1 + 0.1 * gradient
    new_moment2 = 0.95 * moment2 + 0.05 * gradient * gradient
    update = new_moment1 / FIRST_FIX / (jnp.sqrt(new_moment2 / SECOND_FIX) + 1e-08)
    plain = weight.astype(jnp.float32)
    new_weight = (plain - 0.05 * (update + 0.1 * plain)).astype(jnp.bfloat16)
    new_copy = from_behind(new_weight, "section", -lanes)
    return (spare, grad_own, new_weight, new_moment1, new_moment2, new_copy)


def solution(mesh):
    in_specs = (
        P("dp", None),
        P("dp", None),
        P("dp", "section"),
        P("dp", "section"),
        P("dp", "section"),
    )
    out_specs = (
        P("dp", "section"),
        P("dp", "section"),
        P("dp", "section"),
        P("dp", "section"),
        P("dp", "section"),
        P("dp", "section"),
    )
    return jax.shard_map(
        per_device, mesh=mesh, in_specs=in_specs, out_specs=out_specs, check_vma=False
    )
```

profile of v0, /device:TPU:1, one launch (start us, length us, event | category | flops | bytes accessed | tf_op | source)
XLA Modules:
  0.0 535.4 jit_solution(6084127349864773904)
XLA Ops:
  8.3 74.1 %all_gather.6 = bf16[3072,96]{1,0:T(8,128)(2,1)S(1)} all-gather(bf16[384,96]{1,0:T(8,128)(2,1)S(1)} %copy.25), channel_id=1, replica_groups=mesh['section'=64,'dp'=8] {'dp'}, dimensions={0}, use_global_device_ids=true | all-gather | bytes 663552 | tf_op jit(solution)/shard_map/all_gather | solution.py:88
  82.4 2.9 conditional.4
  87.6 9.6 %collective-permute-start.1 = (bf16[128,96]{0,1:T(8,128)(2,1)S(1)}, bf16[128,96]{0,1:T(8,128)(2,1)S(1)}, u32[]{:S(2)}, u32[]{:S(2)}) collective-permute-start(bf16[128,96]{0,1:T(8,128)(2,1)S(1)} %collective-permute-done), channel_id=1, source_target_pairs={{0,8},{8,0},{16,24},{24,16},{32,40},{40,32},{48,56},{56,48},{64,72... | collective-permute-start | bytes 73736 | tf_op jit(solution)/shard_map/ppermute | solution.py:18
  98.1 2.6 collective-permute-start.2
  102.9 4.1 collective-permute-start.3
  107.1 2.7 collective-permute-done.3
  109.9 3.5 collective-permute-start.4
  113.4 3.0 collective-permute-done.4
  116.6 4.4 collective-permute-start.5
  121.9 16.1 %collective-permute-done.5 = bf16[128,1536]{0,1:T(8,128)(2,1)S(1)} collective-permute-done((bf16[128,1536]{0,1:T(8,128)(2,1)S(1)}, bf16[128,1536]{0,1:T(8,128)(2,1)S(1)}, u32[]{:S(2)}, u32[]{:S(2)}) %collective-permute-start.5) | collective-permute-done | bytes 393248 | tf_op jit(solution)/shard_map/ppermute | solution.py:18
  141.9 36.7 %collective-permute-done.12 = f32[128,1536]{0,1:T(8,128)S(1)} collective-permute-done((f32[128,1536]{0,1:T(8,128)S(1)}, f32[128,1536]{0,1:T(8,128)S(1)}, u32[]{:S(2)}, u32[]{:S(2)}) %collective-permute-start.12) | collective-permute-done | bytes 786464 | tf_op jit(solution)/shard_map/ppermute | solution.py:18
  186.3 6.4 %collective-permute-done.13 = f32[128,768]{0,1:T(8,128)S(1)} collective-permute-done((f32[128,768]{0,1:T(8,128)}, f32[128,768]{0,1:T(8,128)S(1)}, u32[]{:S(2)}, u32[]{:S(2)}) %collective-permute-start.13) | collective-permute-done | bytes 393248 | tf_op jit(solution)/shard_map/ppermute | solution.py:18
  192.8 4.0 collective-permute-start.14
  197.3 4.0 collective-permute-done.14
  201.4 2.5 collective-permute-start.15
  203.9 2.8 collective-permute-done.15
  206.8 5.4 %collective-permute-start.16 = (f32[128,96]{0,1:T(8,128)S(1)}, f32[128,96]{0,1:T(8,128)S(1)}, u32[]{:S(2)}, u32[]{:S(2)}) collective-permute-start(f32[128,96]{0,1:T(8,128)S(1)} %slice_select_fusion.7), channel_id=1, source_target_pairs={{0,8},{8,0},{16,24},{24,16},{32,40},{40,32},{48,56},{56,48},{64,72... | collective-permute-start | bytes 147464 | tf_op jit(solution)/shard_map/ppermute | solution.py:18
  218.7 2.5 collective-permute-start.6
  221.3 4.4 collective-permute-start.19
  231.4 2.7 collective-permute-start.21
  238.0 2.8 collective-permute-start.7
  240.8 9.7 %collective-permute-done.22 = bf16[128,96]{0,1:T(8,128)(2,1)S(1)} collective-permute-done((bf16[128,96]{0,1:T(8,128)(2,1)S(1)}, bf16[128,96]{0,1:T(8,128)(2,1)S(1)}, u32[]{:S(2)}, u32[]{:S(2)}) %collective-permute-start.22) | collective-permute-done | bytes 24608 | tf_op jit(solution)/shard_map/ppermute | solution.py:24
  251.1 3.1 conditional.7
  258.2 4.4 collective-permute-start.8
  266.1 3.0 collective-permute-start.9
  269.2 28.0 %collective-permute-done.23 = f32[128,1536]{0,1:T(8,128)} collective-permute-done((f32[128,1536]{0,1:T(8,128)}, f32[128,1536]{0,1:T(8,128)}, u32[]{:S(2)}, u32[]{:S(2)}) %collective-permute-start.23) | collective-permute-done | bytes 786464 | tf_op jit(solution)/shard_map/ppermute | solution.py:18
  300.4 71.5 %all_gather.7 = bf16[3072,96]{0,1:T(8,128)(2,1)S(1)} all-gather(bf16[384,96]{0,1:T(8,128)(2,1)} %collective-permute-done.11), channel_id=1, replica_groups=mesh['section'=64,'dp'=8] {'dp'}, dimensions={0}, use_global_device_ids=true | all-gather | bytes 663552 | tf_op jit(solution)/shard_map/all_gather | solution.py:89
  372.1 6.3 %collective-permute-start.25 = (f32[128,384]{0,1:T(8,128)S(1)}, f32[128,384]{0,1:T(8,128)S(1)}, u32[]{:S(2)}, u32[]{:S(2)}) collective-permute-start(f32[128,384]{0,1:T(8,128)S(1)} %slice_select_fusion.2), channel_id=1, source_target_pairs={{0,32},{8,40},{16,48},{24,56},{32,0},{40,8},{48,16},{56,24},{64,96... | collective-permute-start | bytes 589832 | tf_op jit(solution)/shard_map/ppermute | solution.py:18
  383.5 10.2 %collective-permute-done.10 = bf16[128,1536]{0,1:T(8,128)(2,1)S(1)} collective-permute-done((bf16[128,1536]{0,1:T(8,128)(2,1)S(1)}, bf16[128,1536]{0,1:T(8,128)(2,1)S(1)}, u32[]{:S(2)}, u32[]{:S(2)}) %collective-permute-start.10) | collective-permute-done | bytes 393248 | tf_op jit(solution)/shard_map/ppermute | solution.py:18
  394.3 9.5 %collective-permute-start.27 = (f32[128,96]{0,1:T(8,128)S(1)}, f32[128,96]{0,1:T(8,128)S(1)}, u32[]{:S(2)}, u32[]{:S(2)}) collective-permute-start(f32[128,96]{0,1:T(8,128)S(1)} %slice_select_fusion.6), channel_id=1, source_target_pairs={{0,8},{8,0},{16,24},{24,16},{32,40},{40,32},{48,56},{56,48},{64,72... | collective-permute-start | bytes 147464 | tf_op jit(solution)/shard_map/ppermute | solution.py:18
  417.5 90.5 %reduce-scatter.4.cloned.1.call-done = bf16[384,96]{1,0:T(8,128)(2,1)} async-done(((bf16[3072,96]{1,0:T(8,128)(2,1)}), bf16[384,96]{1,0:T(8,128)(2,1)}) %reduce-scatter.4.cloned.1.call-update) | async-done | bytes 73744
  516.5 9.9 %collective-permute-done.33 = bf16[384,96]{0,1:T(8,128)(2,1)S(1)} collective-permute-done((bf16[384,96]{0,1:T(8,128)(2,1)S(1)}, bf16[384,96]{0,1:T(8,128)(2,1)S(1)}, u32[]{:S(2)}, u32[]{:S(2)}) %collective-permute-start.33) | collective-permute-done | bytes 73760 | tf_op jit(solution)/shard_map/ppermute | solution.py:24
  (178 shorter events, 82.9 us)
Async XLA Ops:
  7.2 500.8 %reduce-scatter.4.cloned.1.call-start = ((), (), s32[]{:S(2)}) async-start(), calls=%async_computation.1 | async-start | bytes 884736
  87.6 10.5 %collective-permute-start.1 = (bf16[128,96]{0,1:T(8,128)(2,1)S(1)}, bf16[128,96]{0,1:T(8,128)(2,1)S(1)}, u32[]{:S(2)}, u32[]{:S(2)}) collective-permute-start(bf16[128,96]{0,1:T(8,128)(2,1)S(1)} %collective-permute-done), channel_id=1, source_target_pairs={{0,8},{8,0},{16,24},{24,16},{32,40},{40,32},{48,56},{56,48},{64,72... | collective-permute-start | bytes 73736 | tf_op jit(solution)/shard_map/ppermute | solution.py:18
  98.1 4.8 collective-permute-start.2
  102.9 6.9 %collective-permute-start.3 = (bf16[128,384]{0,1:T(8,128)(2,1)S(1)}, bf16[128,384]{0,1:T(8,128)(2,1)S(1)}, u32[]{:S(2)}, u32[]{:S(2)}) collective-permute-start(bf16[128,384]{0,1:T(8,128)(2,1)S(1)} %pad_maximum_fusion.7), channel_id=1, source_target_pairs={{0,32},{8,40},{16,48},{24,56},{32,0},{40,8},{48,16},{56,24},{64,96... | collective-permute-start | bytes 294920 | tf_op jit(solution)/shard_map/ppermute | solution.py:18
  109.9 6.6 %collective-permute-start.4 = (bf16[128,768]{0,1:T(8,128)(2,1)S(1)}, bf16[128,768]{0,1:T(8,128)(2,1)S(1)}, u32[]{:S(2)}, u32[]{:S(2)}) collective-permute-start(bf16[128,768]{0,1:T(8,128)(2,1)S(1)} %pad_maximum_fusion.5), channel_id=1, source_target_pairs={{0,64},{8,72},{16,80},{24,88},{32,96},{40,104},{48,112},{56,120},{... | collective-permute-start | bytes 589832 | tf_op jit(solution)/shard_map/ppermute | solution.py:18
  116.6 21.4 %collective-permute-start.5 = (bf16[128,1536]{0,1:T(8,128)(2,1)S(1)}, bf16[128,1536]{0,1:T(8,128)(2,1)S(1)}, u32[]{:S(2)}, u32[]{:S(2)}) collective-permute-start(bf16[128,1536]{0,1:T(8,128)(2,1)S(1)} %pad_maximum_fusion.2), channel_id=1, source_target_pairs={{0,128},{8,136},{16,144},{24,152},{32,160},{40,168},{48,176},{56,1... | collective-permute-start | bytes 1179656 | tf_op jit(solution)/shard_map/ppermute | solution.py:18
  140.0 38.7 %collective-permute-start.12 = (f32[128,1536]{0,1:T(8,128)S(1)}, f32[128,1536]{0,1:T(8,128)S(1)}, u32[]{:S(2)}, u32[]{:S(2)}) collective-permute-start(f32[128,1536]{0,1:T(8,128)S(1)} %broadcast_select_fusion.2), channel_id=1, source_target_pairs={{0,128},{8,136},{16,144},{24,152},{32,160},{40,168},{48,176},{56,1... | collective-permute-start | bytes 2359304 | tf_op jit(solution)/shard_map/ppermute | solution.py:18
  180.5 12.3 %collective-permute-start.13 = (f32[128,768]{0,1:T(8,128)}, f32[128,768]{0,1:T(8,128)S(1)}, u32[]{:S(2)}, u32[]{:S(2)}) collective-permute-start(f32[128,768]{0,1:T(8,128)} %slice_select_fusion.1), channel_id=1, source_target_pairs={{0,64},{8,72},{16,80},{24,88},{32,96},{40,104},{48,112},{56,120},{... | collective-permute-start | bytes 1179656 | tf_op jit(solution)/shard_map/ppermute | solution.py:18
  192.8 8.5 %collective-permute-start.14 = (f32[128,384]{0,1:T(8,128)S(1)}, f32[128,384]{0,1:T(8,128)S(1)}, u32[]{:S(2)}, u32[]{:S(2)}) collective-permute-start(f32[128,384]{0,1:T(8,128)S(1)} %slice_select_fusion.3), channel_id=1, source_target_pairs={{0,32},{8,40},{16,48},{24,56},{32,0},{40,8},{48,16},{56,24},{64,96... | collective-permute-start | bytes 589832 | tf_op jit(solution)/shard_map/ppermute | solution.py:18
  201.4 5.4 %collective-permute-start.15 = (f32[128,192]{0,1:T(8,128)S(1)}, f32[128,192]{0,1:T(8,128)S(1)}, u32[]{:S(2)}, u32[]{:S(2)}) collective-permute-start(f32[128,192]{0,1:T(8,128)S(1)} %slice_select_fusion.5), channel_id=1, source_target_pairs={{0,16},{8,24},{16,0},{24,8},{32,48},{40,56},{48,32},{56,40},{64,80... | collective-permute-start | bytes 294920 | tf_op jit(solution)/shard_map/ppermute | solution.py:18
  206.8 6.3 %collective-permute-start.16 = (f32[128,96]{0,1:T(8,128)S(1)}, f32[128,96]{0,1:T(8,128)S(1)}, u32[]{:S(2)}, u32[]{:S(2)}) collective-permute-start(f32[128,96]{0,1:T(8,128)S(1)} %slice_select_fusion.7), channel_id=1, source_target_pairs={{0,8},{8,0},{16,24},{24,16},{32,40},{40,32},{48,56},{56,48},{64,72... | collective-permute-start | bytes 147464 | tf_op jit(solution)/shard_map/ppermute | solution.py:18
  216.2 5.0 collective-permute-start.18
  218.7 15.4 %collective-permute-start.6 = (bf16[128,96]{0,1:T(8,128)(2,1)S(1)}, bf16[128,96]{0,1:T(8,128)(2,1)S(1)}, u32[]{:S(2)}, u32[]{:S(2)}) collective-permute-start(bf16[128,96]{0,1:T(8,128)(2,1)S(1)} %select_select_fusion), channel_id=1, source_target_pairs={{0,8},{8,0},{16,24},{24,16},{32,40},{40,32},{48,56},{56,48},{64,72... | collective-permute-start | bytes 73736 | tf_op jit(solution)/shard_map/ppermute | solution.py:18
  221.3 5.8 %collective-permute-start.19 = (f32[2,128]{1,0:T(2,128)S(1)}, f32[2,128]{1,0:T(2,128)S(1)}, u32[]{:S(2)}, u32[]{:S(2)}) collective-permute-start(f32[2,128]{1,0:T(2,128)S(1)} %fusion.73), channel_id=1, source_target_pairs={{0,32},{8,40},{16,48},{24,56},{32,0},{40,8},{48,16},{56,24},{64,96... | collective-permute-start | bytes 3080 | tf_op jit(solution)/shard_map/ppermute | solution.py:18
  227.1 4.3 collective-permute-start.20
  231.4 5.2 collective-permute-start.21
  236.7 13.8 %collective-permute-start.22 = (bf16[128,96]{0,1:T(8,128)(2,1)S(1)}, bf16[128,96]{0,1:T(8,128)(2,1)S(1)}, u32[]{:S(2)}, u32[]{:S(2)}) collective-permute-start(bf16[128,96]{0,1:T(8,128)(2,1)S(1)} %fusion.36), channel_id=1, source_target_pairs={{256,0},{264,8},{272,16},{280,24},{288,32},{296,40},{304,48},{312,... | collective-permute-start | bytes 73736 | tf_op jit(solution)/shard_map/ppermute | solution.py:24
  238.0 19.4 %collective-permute-start.7 = (bf16[128,192]{0,1:T(8,128)(2,1)S(1)}, bf16[128,192]{0,1:T(8,128)(2,1)}, u32[]{:S(2)}, u32[]{:S(2)}) collective-permute-start(bf16[128,192]{0,1:T(8,128)(2,1)S(1)} %pad_maximum_fusion.10), channel_id=1, source_target_pairs={{0,16},{8,24},{16,0},{24,8},{32,48},{40,56},{48,32},{56,40},{64,80... | collective-permute-start | bytes 147464 | tf_op jit(solution)/shard_map/ppermute | solution.py:18
  255.2 42.0 %collective-permute-start.23 = (f32[128,1536]{0,1:T(8,128)}, f32[128,1536]{0,1:T(8,128)}, u32[]{:S(2)}, u32[]{:S(2)}) collective-permute-start(f32[128,1536]{0,1:T(8,128)} %broadcast_select_fusion.1), channel_id=1, source_target_pairs={{0,128},{8,136},{16,144},{24,152},{32,160},{40,168},{48,176},{56,1... | collective-permute-start | bytes 2359304 | tf_op jit(solution)/shard_map/ppermute | solution.py:18
  258.2 7.0 %collective-permute-start.8 = (bf16[128,384]{0,1:T(8,128)(2,1)S(1)}, bf16[128,384]{0,1:T(8,128)(2,1)}, u32[]{:S(2)}, u32[]{:S(2)}) collective-permute-start(bf16[128,384]{0,1:T(8,128)(2,1)S(1)} %pad_maximum_fusion.8), channel_id=1, source_target_pairs={{0,32},{8,40},{16,48},{24,56},{32,0},{40,8},{48,16},{56,24},{64,96... | collective-permute-start | bytes 294920 | tf_op jit(solution)/shard_map/ppermute | solution.py:18
  262.6 37.8 %collective-permute-start.11 = (bf16[384,96]{0,1:T(8,128)(2,1)S(1)}, bf16[384,96]{0,1:T(8,128)(2,1)}, u32[]{:S(2)}, u32[]{:S(2)}) collective-permute-start(bf16[384,96]{0,1:T(8,128)(2,1)S(1)} %copy-done.6), channel_id=1, source_target_pairs={{256,0},{264,8},{272,16},{280,24},{288,32},{296,40},{304,48},{312,... | collective-permute-start | bytes 221192 | tf_op jit(solution)/shard_map/ppermute | solution.py:24
  266.1 105.8 %collective-permute-start.9 = (bf16[128,768]{0,1:T(8,128)(2,1)S(1)}, bf16[128,768]{0,1:T(8,128)(2,1)S(1)}, u32[]{:S(2)}, u32[]{:S(2)}) collective-permute-start(bf16[128,768]{0,1:T(8,128)(2,1)S(1)} %pad_maximum_fusion.6), channel_id=1, source_target_pairs={{0,64},{8,72},{16,80},{24,88},{32,96},{40,104},{48,112},{56,120},{... | collective-permute-start | bytes 589832 | tf_op jit(solution)/shard_map/ppermute | solution.py:18
  298.5 73.5 %collective-permute-start.24 = (f32[128,768]{0,1:T(8,128)S(1)}, f32[128,768]{0,1:T(8,128)S(1)}, u32[]{:S(2)}, u32[]{:S(2)}) collective-permute-start(f32[128,768]{0,1:T(8,128)S(1)} %slice_select_fusion), channel_id=1, source_target_pairs={{0,64},{8,72},{16,80},{24,88},{32,96},{40,104},{48,112},{56,120},{... | collective-permute-start | bytes 1179656 | tf_op jit(solution)/shard_map/ppermute | solution.py:18
  372.1 9.4 %collective-permute-start.25 = (f32[128,384]{0,1:T(8,128)S(1)}, f32[128,384]{0,1:T(8,128)S(1)}, u32[]{:S(2)}, u32[]{:S(2)}) collective-permute-start(f32[128,384]{0,1:T(8,128)S(1)} %slice_select_fusion.2), channel_id=1, source_target_pairs={{0,32},{8,40},{16,48},{24,56},{32,0},{40,8},{48,16},{56,24},{64,96... | collective-permute-start | bytes 589832 | tf_op jit(solution)/shard_map/ppermute | solution.py:18
  378.5 15.2 %collective-permute-start.10 = (bf16[128,1536]{0,1:T(8,128)(2,1)S(1)}, bf16[128,1536]{0,1:T(8,128)(2,1)S(1)}, u32[]{:S(2)}, u32[]{:S(2)}) collective-permute-start(bf16[128,1536]{0,1:T(8,128)(2,1)S(1)} %pad_maximum_fusion.3), channel_id=1, source_target_pairs={{0,128},{8,136},{16,144},{24,152},{32,160},{40,168},{48,176},{56,1... | collective-permute-start | bytes 1179656 | tf_op jit(solution)/shard_map/ppermute | solution.py:18
  381.6 12.7 %collective-permute-start.26 = (f32[128,192]{0,1:T(8,128)S(1)}, f32[128,192]{0,1:T(8,128)S(1)}, u32[]{:S(2)}, u32[]{:S(2)}) collective-permute-start(f32[128,192]{0,1:T(8,128)S(1)} %slice_select_fusion.4), channel_id=1, source_target_pairs={{0,16},{8,24},{16,0},{24,8},{32,48},{40,56},{48,32},{56,40},{64,80... | collective-permute-start | bytes 294920 | tf_op jit(solution)/shard_map/ppermute | solution.py:18
  394.3 13.0 %collective-permute-start.27 = (f32[128,96]{0,1:T(8,128)S(1)}, f32[128,96]{0,1:T(8,128)S(1)}, u32[]{:S(2)}, u32[]{:S(2)}) collective-permute-start(f32[128,96]{0,1:T(8,128)S(1)} %slice_select_fusion.6), channel_id=1, source_target_pairs={{0,8},{8,0},{16,24},{24,16},{32,40},{40,32},{48,56},{56,48},{64,72... | collective-permute-start | bytes 147464 | tf_op jit(solution)/shard_map/ppermute | solution.py:18
  411.2 4.3 collective-permute-start.29
  415.5 93.4 %collective-permute-start.30 = (f32[2,128]{1,0:T(2,128)S(1)}, f32[2,128]{1,0:T(2,128)S(1)}, u32[]{:S(2)}, u32[]{:S(2)}) collective-permute-start(f32[2,128]{1,0:T(2,128)S(1)} %fusion.72), channel_id=1, source_target_pairs={{0,32},{8,40},{16,48},{24,56},{32,0},{40,8},{48,16},{56,24},{64,96... | collective-permute-start | bytes 3080 | tf_op jit(solution)/shard_map/ppermute | solution.py:18
  509.0 4.3 collective-permute-start.31
  511.8 14.7 %collective-permute-start.33 = (bf16[384,96]{0,1:T(8,128)(2,1)S(1)}, bf16[384,96]{0,1:T(8,128)(2,1)S(1)}, u32[]{:S(2)}, u32[]{:S(2)}) collective-permute-start(bf16[384,96]{0,1:T(8,128)(2,1)S(1)} %get-tuple-element.157), channel_id=1, source_target_pairs={{256,0},{264,8},{272,16},{280,24},{288,32},{296,40},{304,48},{312,... | collective-permute-start | bytes 221192 | tf_op jit(solution)/shard_map/ppermute | solution.py:24
  513.3 13.2 %collective-permute-start.32 = (f32[2,128]{1,0:T(2,128)S(1)}, f32[2,128]{1,0:T(2,128)S(1)}, u32[]{:S(2)}, u32[]{:S(2)}) collective-permute-start(f32[2,128]{1,0:T(2,128)S(1)} %add.227), channel_id=1, source_target_pairs={{0,128},{8,136},{16,144},{24,152},{32,160},{40,168},{48,176},{56,1... | collective-permute-start | bytes 3080 | tf_op jit(solution)/shard_map/ppermute | solution.py:18
  (24 other events, 596.4 us)
Sparse Core Ops, SparseCore 0:
  407.4 100.4 reduce-scatter.3
where the time goes:
time: 537 us; the launch traced here: 535 us
  waiting for transfers between devices  237 us (44%)
  blocking collectives  146 us (27%)
  starting transfers between devices  106 us (20%)
  between operations  15.1 us (3%)
  local copies, waits for them, and re-layouts  14.8 us (3%)
  other arithmetic  14 us (3%)
    ppermute x30, waiting for transfers between devices, swapped(): lax.ppermute(shard, axis, [(i, i ^ 1 << stride) for i in range(lax.axis_s...  126 us
    ppermute x30, starting transfers between devices, swapped(): lax.ppermute(shard, axis, [(i, i ^ 1 << stride) for i in range(lax.axis_s...  100 us
    unnamed x2, waiting for transfers between devices  90.5 us
    all_gather x1, blocking collectives, per_device(): lax.all_gather(weight, 'dp', axis=0, tiled=True)  74.1 us
    all_gather x1, blocking collectives, per_device(): lax.all_gather(successor, 'dp', axis=0, tiled=True)  71.5 us
    ppermute x4, waiting for transfers between devices, from_behind(): return lax.ppermute(shard, axis, pairs)  20.6 us
  transfers between devices with their start and end apart: 35, of which 25 were waited for; matrix products, arithmetic and copies ran while one was open for 4% of the time, Pallas kernels for 0%

commit v1 on v0

v1 whole, which is shorter than its diff:
```python
import math

import jax
import jax.numpy as jnp
from jax import lax
from jax.experimental import pallas as pl
from jax.experimental.pallas import tpu as pltpu
from jax.sharding import PartitionSpec as P

D = 3072
SECTIONS = 2
NORM_EPS = 1e-05
FIRST_FIX = 0.6513215599
SECOND_FIX = 0.4012630607
SCALE = 1.0 / math.sqrt(D)
HALF = 64
LANE = 96
PAIR = 192
WIDE = 256
ROWS = 384
F32 = jnp.float32
BF16 = jnp.bfloat16

W_Z, W_Y, W_ZY, W_C = 0, 1, 4, 7
X_UP, X_Z, X_X = 15, 16, 19
LOW, X2, SPARE, SLOPE = 31, 32, 33, 34
B_X, B_Z = 35, 47
G_DOWN, G_C = 50, 51
G_YO, G_YS, G_Z, COPY = 52, 55, 58, 59
SLOTS = 60


def gelu_both(z):
    cdf = 0.5 * (1.0 + lax.erf(z * 0.7071067811865476))
    return z * cdf, cdf + z * jnp.exp(-0.5 * z * z) * 0.3989422804014327


def kernel(
    inputs, cotangent, w, m1, m2,
    spare, grad, new_w, new_m1, new_m2, copy,
    xin, cot, wv, m1v, m2v, wp, csum, low, xg, xout, normed, inv, mixed, slope_of, up, g_in,
    slope_t, sl, x2_t, x2, spare_in, bsend, brecv, zacc, zsend, zrecv,
    gout, g_t, gc, gsend, grecv, gzs, gzr, copy_out, copy_in,
    send_sem, recv_sem, here_sem,
):
    sec = lax.axis_index("section")
    dp = lax.axis_index("dp")
    c = sec % 2
    x = sec // 2 % 4
    s = sec // 32
    zq = sec // 8 % 4
    y = dp % 4
    zh = dp // 4
    odd = x % 2
    other = dp + 4 - 8 * zh
    core = {"section": sec + 1 - 2 * c, "dp": dp}
    across = {"section": sec + 32 - 64 * s, "dp": dp}
    far = {"section": sec, "dp": other}
    ys = [{"section": sec, "dp": zh * 4 + (y + j) % 4} for j in (1, 2, 3)]
    xs = [{"section": s * 32 + zq * 8 + (x + j) % 4 * 2 + c, "dp": dp} for j in (1, 2, 3)]
    zs = [{"section": s * 32 + (zq + j) % 4 * 8 + x * 2 + c, "dp": dp} for j in (1, 2, 3)]
    first = s == 0
    second = s == 1
    window = pl.ds(pl.multiple_of(zq * 768 + x // 2 * 384 + odd * 128, 128), WIDE)
    my_rows = pl.ds(pl.multiple_of(odd * 64 + c * LANE, 32), LANE)
    core_rows = pl.ds(pl.multiple_of(odd * 64 + (1 - c) * LANE, 32), LANE)

    def copier(slot, src, dst, to):
        return pltpu.make_async_remote_copy(
            src_ref=src,
            dst_ref=dst,
            send_sem=send_sem.at[slot],
            recv_sem=recv_sem.at[slot],
            device_id=to,
            device_id_type=pl.DeviceIdType.MESH,
        )

    def arrived(slot, where):
        copier(slot, where, where, core).wait_recv()

    def cols_of(replica):
        return pl.ds(pl.multiple_of(replica * ROWS, ROWS), ROWS)

    load_w = pltpu.make_async_copy(w, wv, here_sem.at[0])
    load_m1 = pltpu.make_async_copy(m1, m1v, here_sem.at[1])
    load_m2 = pltpu.make_async_copy(m2, m2v, here_sem.at[2])
    tokens = [pl.ds(pl.multiple_of(half * HALF, HALF), HALF) for half in (c, 1 - c)]
    load_x = [
        pltpu.make_async_copy(inputs.at[tokens[i]], xin.at[half], here_sem.at[3 + i])
        for i, half in enumerate((c, 1 - c))
    ]
    load_cot = pltpu.make_async_copy(cotangent.at[tokens[0], window], cot, here_sem.at[5])
    load_w.start()

    @pl.when(first)
    def _():
        for one in load_x:
            one.start()

    @pl.when(second)
    def _():
        load_cot.start()

    load_m1.start()
    load_m2.start()

    barrier = pltpu.get_barrier_semaphore()
    peers = [core, across, far] + ys + xs + zs
    for peer in peers:
        pl.semaphore_signal(barrier, inc=1, device_id=peer, device_id_type=pl.DeviceIdType.MESH)
    load_w.wait()
    pl.semaphore_wait(barrier, len(peers))

    mine = wp.at[my_rows, cols_of(dp)]
    sent = [copier(W_Z, wv, mine, far)]
    sent += [copier(W_Y + j, wv, mine, ys[j]) for j in range(3)]
    sent.append(copier(W_C, wv, mine, core))
    for one in sent:
        one.start()
    wp[my_rows, cols_of(dp)] = wv[...]
    blank = pl.ds(pl.multiple_of((1 - odd) * PAIR, 64), WIDE - PAIR)
    wp[blank, :] = jnp.zeros((WIDE - PAIR, D), BF16)

    def normalise(rows):
        centre = jnp.mean(rows, axis=1, keepdims=True)
        gap = rows - centre
        scale = lax.rsqrt(jnp.mean(gap * gap, axis=1, keepdims=True) + NORM_EPS)
        return (gap * scale).astype(BF16), centre, scale

    def keep_stats(block, centre, scale):
        inv[...] = jnp.broadcast_to(scale, (HALF, 128))
        normed[...] = (block.astype(F32) - centre) * scale

    @pl.when(first)
    def _():
        load_x[0].wait()
        low[c], centre, scale = normalise(xin[c].astype(F32))
        keep_stats(xin[c, :, window], centre, scale)

    def to_core(slot, replica):
        block = wp.at[my_rows, cols_of(replica)]
        one = copier(slot, block, block, core)
        one.start()
        sent.append(one)

    from_y = [zh * 4 + (y + 4 - j) % 4 for j in (1, 2, 3)]
    from_zy = [(1 - zh) * 4 + (y + 4 - j) % 4 for j in (1, 2, 3)]
    held = wp.at[my_rows, cols_of(other)]
    arrived(W_Z, held)
    for j in range(3):
        one = copier(W_ZY + j, held, held, ys[j])
        one.start()
        sent.append(one)
    to_core(W_C + 1, other)
    for j in range(3):
        arrived(W_Y + j, wp.at[my_rows, cols_of(from_y[j])])
        to_core(W_C + 2 + j, from_y[j])
    for j in range(3):
        arrived(W_ZY + j, wp.at[my_rows, cols_of(from_zy[j])])
        to_core(W_C + 5 + j, from_zy[j])
    for i, replica in enumerate([dp, other] + from_y + from_zy):
        arrived(W_C + i, wp.at[core_rows, cols_of(replica)])

    def column_sums():
        csum[...] = lax.dot_general(
            jnp.ones((16, D), BF16), wp[...], (((1,), (1,)), ((), ())), preferred_element_type=F32
        )

    own = xg.at[x, zq]
    x_up = copier(X_UP, xout, own, across)
    x_z = [copier(X_Z + j, own, own, zs[j]) for j in range(3)]
    x_x = []
    for i in range(4):
        block = xg.at[x, (zq + 4 - i) % 4]
        x_x.append([copier(X_X + 3 * i + j, block, block, xs[j]) for j in range(3)])
    swap_low = copier(LOW, low.at[c], low.at[c], core)

    @pl.when(second)
    def _():
        column_sums()
        arrived(X_UP, own)
        for one in x_z + x_x[0]:
            one.start()
        for j in range(3):
            arrived(X_Z + j, xg.at[x, (zq + 3 - j) % 4])
            for one in x_x[j + 1]:
                one.start()
        for i in range(4):
            for j in range(3):
                arrived(X_X + 3 * i + j, xg.at[(x + 3 - j) % 4, (zq + 4 - i) % 4])
        left = lax.broadcasted_iota(jnp.int32, (HALF, 128), 1) < HALF
        parts = []
        for m in range(8):
            even = xg[m % 2 * 2, m // 2].astype(F32)
            late = xg[m % 2 * 2 + 1, m // 2].astype(F32)
            middle = jnp.where(left, even[:, 128:], late[:, :128])
            parts += [even[:, :128], middle, late[:, 128:]]
        low[c], centre, scale = normalise(jnp.concatenate(parts, axis=1))
        swap_low.start()
        keep_stats(xg[x, zq], centre, scale)
        load_cot.wait()
        up[...] = cot[...].astype(F32)

    z = SCALE * lax.dot_general(
        low[c], wp[...], (((1,), (1,)), ((), ())), preferred_element_type=F32
    )
    value, slope_value = gelu_both(z)
    mixed[...] = z
    slope_of[...] = slope_value

    @pl.when(first)
    def _():
        xout[...] = (xin[c, :, window].astype(F32) + value).astype(BF16)
        x_up.start()
        load_x[1].wait()
        low[1 - c], _, _ = normalise(xin[1 - c].astype(F32))
        column_sums()
        arrived(G_DOWN, g_in)
        up[...] = g_in[...].astype(F32)

    slope = (up[...] * slope_of[...]).astype(BF16)
    swap_slope = copier(SLOPE, slope_t.at[core_rows], sl.at[c], core)
    b_x = []
    for i in range(4):
        q = (zq + 1 + i) % 4
        b_x.append(
            [copier(B_X + 3 * i + j, bsend.at[(x + 1 + j) % 4, q], brecv.at[j, q], xs[j])
             for j in range(3)]
        )

    def give_slope():
        slope_t[...] = slope.T
        swap_slope.start()
        sl[c] = slope_t[my_rows, :]

    def back():
        wide = slope.astype(F32)
        r1 = jnp.sum(wide * csum[0:1, :], axis=1, keepdims=True) * (SCALE / D)
        r2 = jnp.sum(wide * mixed[...], axis=1, keepdims=True) * (1.0 / D)
        h1 = r1.astype(BF16).astype(F32)
        h2 = r2.astype(BF16).astype(F32)
        lane = lax.broadcasted_iota(jnp.int32, (HALF, 128), 1)
        spot = lane % 64
        sums = jnp.where(
            spot == 0, h1, jnp.where(spot == 1, r1 - h1, jnp.where(spot == 2, h2, r2 - h2))
        )
        for i in range(4):
            q = (zq + 1 + i) % 4
            for half in range(2):
                cols = pl.ds(pl.multiple_of(q * 768 + half * 384, 384), 384)
                part = SCALE * jnp.dot(slope, wp[:, cols], preferred_element_type=F32)
                middle = part[:, 128:256]
                bsend[2 * half, q, :, :128] = part[:, :128].astype(BF16)
                bsend[2 * half, q, :, 128:] = jnp.where(lane < 64, middle, sums).astype(BF16)
                bsend[2 * half + 1, q, :, :128] = jnp.where(lane < 64, sums, middle).astype(BF16)
                bsend[2 * half + 1, q, :, 128:] = part[:, 256:].astype(BF16)
            for one in b_x[i]:
                one.start()

    swap_x2 = copier(X2, x2_t.at[core_rows], x2.at[c], core)

    @pl.when(second)
    def _():
        back()
        give_slope()
        x2_t[...] = (xg[x, zq].astype(F32) + value).astype(BF16).T
        swap_x2.start()
        x2[c] = x2_t[my_rows, :]
        arrived(LOW, low.at[1 - c])

    @pl.when(first)
    def _():
        give_slope()

    arrived(SLOPE, sl.at[1 - c])
    whole = jnp.concatenate([sl[0], sl[1]], axis=1)
    g_y = []
    for i, half in enumerate((1 - zh, zh)):
        for j in range(4):
            to = (y + 1 + j) % 4
            cols = cols_of(half * 4 + to)
            rows = low[:, :, cols].reshape(2 * HALF, ROWS)
            part = jnp.dot(whole, rows, preferred_element_type=F32)
            gsend[half, to] = (part * SCALE).astype(BF16)
            if j < 3:
                one = copier(G_YO + 3 * i + j, gsend.at[half, to], grecv.at[i, j], ys[j])
                one.start()
                g_y.append(one)

    @pl.when(first)
    def _():
        back()

    b_z = []
    for i in range(4):
        q = (zq + 1 + i) % 4
        total = bsend[x, q].astype(F32)
        for j in range(3):
            arrived(B_X + 3 * i + j, brecv.at[j, q])
            total = total + brecv[j, q].astype(F32)
        if i < 3:
            zsend[q] = total.astype(BF16)
            one = copier(B_Z + i, zsend.at[q], zrecv.at[i], zs[i])
            one.start()
            b_z.append(one)
        else:
            zacc[...] = total

    send_far = copier(G_Z, gzs, gzr, far)

    def reduce_far():
        total = gsend[1 - zh, y].astype(F32)
        for j in range(3):
            arrived(G_YO + j, grecv.at[0, j])
            total = total + grecv[0, j].astype(F32)
        gzs[...] = total.astype(BF16)
        send_far.start()

    @pl.when(first)
    def _():
        reduce_far()

    total = zacc[...]
    for j in range(3):
        arrived(B_Z + j, zrecv.at[j])
        total = total + zrecv[j].astype(F32)
    tail = jnp.where(odd == 0, total[:, PAIR:], total[:, : WIDE - PAIR])
    r1 = tail[:, 0:1] + tail[:, 1:2]
    r2 = tail[:, 2:3] + tail[:, 3:4]
    change = inv[:, 0:1] * (total - r1 - normed[...] * r2)
    renewed = (up[...] + change).astype(BF16)
    gout[...] = renewed
    g_down = copier(G_DOWN, gout, g_in, across)

    @pl.when(second)
    def _():
        g_down.start()

    g_t[...] = renewed.T
    swap_g = copier(G_C, g_t.at[core_rows], gc.at[c], core)
    swap_g.start()
    gc[c] = g_t[my_rows, :]

    send_spare = copier(SPARE, x2, spare_in, across)

    @pl.when(second)
    def _():
        reduce_far()
        arrived(X2, x2.at[1 - c])
        send_spare.start()

    total = gsend[zh, y].astype(F32)
    for j in range(3):
        arrived(G_YS + j, grecv.at[1, j])
        total = total + grecv[1, j].astype(F32)
    load_m1.wait()
    load_m2.wait()
    arrived(G_Z, gzr)
    gradient = total + gzr[...].astype(F32)
    moment1 = 0.9 * m1v[...] + 0.1 * gradient
    moment2 = 0.95 * m2v[...] + 0.05 * gradient * gradient
    update = moment1 / FIRST_FIX / (jnp.sqrt(moment2 / SECOND_FIX) + 1e-08)
    plain = wv[...].astype(F32)
    stepped = (plain - 0.05 * (update + 0.1 * plain)).astype(BF16)
    copy_out[...] = stepped
    send_copy = copier(COPY, copy_out, copy_in, across)

    @pl.when(second)
    def _():
        send_copy.start()
        spare[...] = jnp.zeros_like(spare)
        copy[...] = jnp.zeros_like(copy)

    new_m1[...] = moment1
    new_m2[...] = moment2
    new_w[...] = stepped

    arrived(G_C, gc.at[1 - c])
    grad[...] = jnp.concatenate([gc[0], gc[1]], axis=1)

    @pl.when(first)
    def _():
        arrived(SPARE, spare_in)
        spare[...] = jnp.concatenate([spare_in[0], spare_in[1]], axis=1)
        arrived(COPY, copy_in)
        copy[...] = copy_in[...]
        x_up.wait_send()

    for one in sent + [swap_slope, swap_g, send_far] + sum(b_x, []) + b_z + g_y:
        one.wait_send()

    @pl.when(second)
    def _():
        for one in x_z + sum(x_x, []) + [swap_low, swap_x2, g_down, send_spare, send_copy]:
            one.wait_send()


def per_device(inputs, cotangent, weight, moment1, moment2):
    vmem = pl.BlockSpec(memory_space=pltpu.VMEM)
    anywhere = pl.BlockSpec(memory_space=pl.ANY)
    shape = jax.ShapeDtypeStruct
    outs = [
        shape((LANE, 2 * HALF), BF16),
        shape((LANE, 2 * HALF), BF16),
        shape((LANE, ROWS), BF16),
        shape((LANE, ROWS), F32),
        shape((LANE, ROWS), F32),
        shape((LANE, ROWS), BF16),
    ]
    scratch = [
        ((2, HALF, D), BF16),
        ((HALF, WIDE), BF16),
        ((LANE, ROWS), BF16),
        ((LANE, ROWS), F32),
        ((LANE, ROWS), F32),
        ((WIDE, D), BF16),
        ((16, WIDE), F32),
        ((2, HALF, D), BF16),
        ((4, 4, HALF, WIDE), BF16),
        ((HALF, WIDE), BF16),
        ((HALF, WIDE), F32),
        ((HALF, 128), F32),
        ((HALF, WIDE), F32),
        ((HALF, WIDE), F32),
        ((HALF, WIDE), F32),
        ((HALF, WIDE), BF16),
        ((WIDE, HALF), BF16),
        ((2, LANE, HALF), BF16),
        ((WIDE, HALF), BF16),
        ((2, LANE, HALF), BF16),
        ((2, LANE, HALF), BF16),
        ((4, 4, HALF, WIDE), BF16),
        ((3, 4, HALF, WIDE), BF16),
        ((HALF, WIDE), F32),
        ((4, HALF, WIDE), BF16),
        ((3, HALF, WIDE), BF16),
        ((HALF, WIDE), BF16),
        ((WIDE, HALF), BF16),
        ((2, LANE, HALF), BF16),
        ((2, 4, LANE, ROWS), BF16),
        ((2, 3, LANE, ROWS), BF16),
        ((LANE, ROWS), BF16),
        ((LANE, ROWS), BF16),
        ((LANE, ROWS), BF16),
        ((LANE, ROWS), BF16),
    ]
    results = pl.pallas_call(
        kernel,
        out_shape=outs,
        in_specs=[anywhere] * 5,
        out_specs=[vmem] * 6,
        scratch_shapes=[pltpu.VMEM(dims, kind) for dims, kind in scratch]
        + [pltpu.SemaphoreType.DMA((SLOTS,))] * 2
        + [pltpu.SemaphoreType.DMA((6,))],
        compiler_params=pltpu.CompilerParams(
            collective_id=0, has_side_effects=True, vmem_limit_bytes=40 * 2**20
        ),
    )(inputs, cotangent, weight.T, moment1.T, moment2.T)
    return tuple(one.T for one in results)


def solution(mesh):
    split = P("dp", "section")
    return jax.shard_map(
        per_device,
        mesh=mesh,
        in_specs=(P("dp", None), P("dp", None), split, split, split),
        out_specs=(split,) * 6,
        check_vma=False,
    )
```

time: 537 us -> 107 us (0.20)
  waiting for transfers between devices: 237 us -> 0 us
  blocking collectives: 146 us -> 0 us
  starting transfers between devices: 106 us -> 0 us
  Pallas kernels: 0 us -> 97.1 us
  between operations: 15.1 us -> 0.66 us
  other arithmetic: 14 us -> 0 us
  local copies, waits for them, and re-layouts: 14.8 us -> 8.76 us
    ppermute x34 -> x0, waiting for transfers between devices: 147 us -> none  [the longest x30 126 us: swapped(): lax.ppermute(shard, axis, [(i, i ^ 1 << stride) for i in range(lax.axis_s...]
    all_gather x2 -> x0, blocking collectives: 146 us -> none  [the longest x1 74.1 us: per_device(): lax.all_gather(weight, 'dp', axis=0, tiled=True)]
    ppermute x34 -> x0, starting transfers between devices: 106 us -> none  [the longest x30 100 us: swapped(): lax.ppermute(shard, axis, [(i, i ^ 1 << stride) for i in range(lax.axis_s...]
    pallas_call x0 -> x1, Pallas kernels: none -> 97.1 us  [per_device(): pl.pallas_call(kernel, out_shape=outs, in_specs=[anywhere] * 5, out_specs...]
    unnamed x2 -> x0, waiting for transfers between devices: 90.5 us -> none
    select_n x22 -> x0, other arithmetic: 5.77 us -> none  [the longest x10 2.31 us: spread_lanes(): first = jnp.where(upper, other, piece)]
  transfers between devices with their start and end apart: 35 -> 0, of which waited for: 25 -> 0; matrix products, arithmetic and copies ran while one was open for 4% -> 0% of each run, Pallas kernels for 0% -> 0%
where the time goes in v1:
time: 107 us; the launch traced here: 106 us
  Pallas kernels  97.1 us (91%)
  local copies, waits for them, and re-layouts  8.76 us (8%)
    pallas_call x1, Pallas kernels, per_device(): pl.pallas_call(kernel, out_shape=outs, in_specs=[anywhere] * 5, out_specs...  97.1 us
    unnamed x16, local copies, waits for them, and re-layouts  8.76 us

profile of v1, /device:TPU:1, one launch (start us, length us, event | category | flops | bytes accessed | tf_op | source)
XLA Modules:
  0.0 106.5 jit_solution(5418618070175461399)
XLA Ops:
  0.6 0.0 copy-start
  0.6 1.1 %copy-done = bf16[128,3072]{1,0:T(8,128)(2,1)S(1)} copy-done((bf16[128,3072]{1,0:T(8,128)(2,1)S(1)}, bf16[128,3072]{1,0:T(8,128)(2,1)}, u32[]{:S(2)}) %copy-start) | copy-done | bytes 786456
  1.8 0.0 copy-start.1
  1.8 1.1 %copy-done.1 = bf16[128,3072]{1,0:T(8,128)(2,1)S(1)} copy-done((bf16[128,3072]{1,0:T(8,128)(2,1)S(1)}, bf16[128,3072]{1,0:T(8,128)(2,1)}, u32[]{:S(2)}) %copy-start.1) | copy-done | bytes 786456
  2.9 0.0 copy-start.2
  2.9 0.9 copy-done.2
  3.8 0.0 copy-start.3
  3.8 0.9 copy-done.3
  4.7 0.0 copy-start.4
  4.7 0.9 copy-done.4
  5.6 97.1 %shard_map.100 = (bf16[96,128]{1,0:T(8,128)(2,1)S(1)}, bf16[96,128]{1,0:T(8,128)(2,1)S(1)}, bf16[96,384]{1,0:T(8,128)(2,1)S(1)}, f32[96,384]{1,0:T(8,128)S(1)}, ...) custom-call(bf16[128,3072]{1,0:T(8,128)(2,1)S(1)} %copy-done, bf16[128,3072]{1,0:T(8,128)(2,1)S(1)} %copy-done.1, ...), custom_call_target="tpu_custom_call" | custom-call | tf_op jit(solution)/shard_map/pallas_call | solution.py:447
  102.7 0.6 copy.17
  103.3 0.6 copy.18
  103.9 0.6 copy.19
  104.5 0.7 copy.20
  105.2 0.7 copy.21
  105.9 0.6 copy.22
Async XLA Ops:
  0.6 1.1 %copy-start = (bf16[128,3072]{1,0:T(8,128)(2,1)S(1)}, bf16[128,3072]{1,0:T(8,128)(2,1)}, u32[]{:S(2)}) copy-start(bf16[128,3072]{1,0:T(8,128)(2,1)} %inputs.1) | copy-start | bytes 2359300
  1.8 1.1 %copy-start.1 = (bf16[128,3072]{1,0:T(8,128)(2,1)S(1)}, bf16[128,3072]{1,0:T(8,128)(2,1)}, u32[]{:S(2)}) copy-start(bf16[128,3072]{1,0:T(8,128)(2,1)} %cotangent.1) | copy-start | bytes 2359300
  2.9 0.9 copy-start.2
  3.8 0.9 copy-start.3
  4.7 0.9 copy-start.4

commit v2 on v1

v2 whole, which is shorter than its diff:
```python
import math

import jax
import jax.numpy as jnp
from jax import lax
from jax.experimental import pallas as pl
from jax.experimental.pallas import tpu as pltpu
from jax.sharding import PartitionSpec as P

D = 3072
SECTIONS = 2
NORM_EPS = 1e-05
FIRST_FIX = 0.6513215599
SECOND_FIX = 0.4012630607
SCALE = 1.0 / math.sqrt(D)
HALF = 64
LANE = 96
PAIR = 192
WIDE = 256
ROWS = 384
F32 = jnp.float32
BF16 = jnp.bfloat16

PIECE = HALF // 2
CUT = LANE // 2

W_Z, W_Y, W_ZY, W_C = 0, 2, 5, 11
X_UP, X_Z, X_X = 19, 21, 27
LOW, X2, SPARE, SLOPE = 51, 52, 53, 54
B_X, B_Z = 55, 79
G_DOWN, G_C = 85, 87
G_YO, G_YS, G_Z, COPY = 88, 94, 97, 99
SLOTS = 100


def gelu_both(z):
    cdf = 0.5 * (1.0 + lax.erf(z * 0.7071067811865476))
    return z * cdf, cdf + z * jnp.exp(-0.5 * z * z) * 0.3989422804014327


def kernel(
    inputs, cotangent, w, m1, m2,
    spare, grad, new_w, new_m1, new_m2, copy,
    xin, cot, wv, m1v, m2v, wp, csum, low, xg, xout, normed, inv, mixed, slope_of, up, g_in,
    slope_t, sl, x2_t, x2, spare_in, bsend, brecv, zacc, zsend, zrecv,
    gout, g_t, gc, gsend, grecv, gzs, gzr, copy_out, copy_in, slopes, x2_w,
    send_sem, recv_sem, here_sem, go,
):
    sec = lax.axis_index("section")
    dp = lax.axis_index("dp")
    c = sec % 2
    x = sec // 2 % 4
    s = sec // 32
    zq = sec // 8 % 4
    y = dp % 4
    zh = dp // 4
    odd = x % 2
    other = dp + 4 - 8 * zh
    core = {"section": sec + 1 - 2 * c, "dp": dp}
    across = {"section": sec + 32 - 64 * s, "dp": dp}
    far = {"section": sec, "dp": other}
    ys = [{"section": sec, "dp": zh * 4 + (y + j) % 4} for j in (1, 2, 3)]
    xs = [{"section": s * 32 + zq * 8 + (x + j) % 4 * 2 + c, "dp": dp} for j in (1, 2, 3)]
    zs = [{"section": s * 32 + (zq + j) % 4 * 8 + x * 2 + c, "dp": dp} for j in (1, 2, 3)]
    first = s == 0
    second = s == 1
    window = pl.ds(pl.multiple_of(zq * 768 + x // 2 * 384 + odd * 128, 128), WIDE)
    my_rows = pl.ds(pl.multiple_of(odd * 64 + c * LANE, 32), LANE)
    core_rows = pl.ds(pl.multiple_of(odd * 64 + (1 - c) * LANE, 32), LANE)

    def copier(slot, src, dst, to):
        return pltpu.make_async_remote_copy(
            src_ref=src,
            dst_ref=dst,
            send_sem=send_sem.at[slot],
            recv_sem=recv_sem.at[slot],
            device_id=to,
            device_id_type=pl.DeviceIdType.MESH,
        )

    def arrived(slot, where):
        copier(slot, where, where, core).wait_recv()

    def cols_of(replica):
        return pl.ds(pl.multiple_of(replica * ROWS, ROWS), ROWS)

    load_w = pltpu.make_async_copy(w, wv, here_sem.at[0])
    load_m1 = pltpu.make_async_copy(m1, m1v, here_sem.at[1])
    load_m2 = pltpu.make_async_copy(m2, m2v, here_sem.at[2])
    tokens = [pl.ds(pl.multiple_of(half * HALF, HALF), HALF) for half in (c, 1 - c)]
    load_x = [
        pltpu.make_async_copy(inputs.at[tokens[i]], xin.at[half], here_sem.at[3 + i])
        for i, half in enumerate((c, 1 - c))
    ]
    load_cot = pltpu.make_async_copy(cotangent.at[tokens[0], window], cot, here_sem.at[5])
    load_w.start()

    @pl.when(first)
    def _():
        for one in load_x:
            one.start()

    @pl.when(second)
    def _():
        load_cot.start()

    load_m1.start()
    load_m2.start()

    barrier = pltpu.get_barrier_semaphore()
    peers = [core, across, far] + ys + xs + zs
    for peer in peers:
        pl.semaphore_signal(barrier, inc=1, device_id=peer, device_id_type=pl.DeviceIdType.MESH)
    load_w.wait()
    pl.semaphore_wait(barrier, len(peers))

    pieces = [pl.ds(PIECE * t, PIECE) for t in range(2)]
    cuts = [pl.ds(CUT * t, CUT) for t in range(2)]
    my_cuts = [pl.ds(pl.multiple_of(odd * 64 + c * LANE + CUT * t, 16), CUT) for t in range(2)]

    w_far = [copier(W_Z + t, wv.at[cuts[t]], wp.at[my_cuts[t], cols_of(dp)], far) for t in range(2)]
    mine = wp.at[my_rows, cols_of(dp)]
    sent = [copier(W_Y + j, wv, mine, ys[j]) for j in range(3)]
    sent.append(copier(W_C, wv, mine, core))

    @pl.when(first)
    def _():
        for one in w_far:
            one.start()

    for one in sent:
        one.start()
    sent += w_far
    wp[my_rows, cols_of(dp)] = wv[...]
    blank = pl.ds(pl.multiple_of((1 - odd) * PAIR, 64), WIDE - PAIR)
    wp[blank, :] = jnp.zeros((WIDE - PAIR, D), BF16)

    def normalise(rows):
        centre = jnp.mean(rows, axis=1, keepdims=True)
        gap = rows - centre
        scale = lax.rsqrt(jnp.mean(gap * gap, axis=1, keepdims=True) + NORM_EPS)
        return (gap * scale).astype(BF16), centre, scale

    def keep_stats(rows, block, centre, scale):
        inv[rows, :] = jnp.broadcast_to(scale, (scale.shape[0], 128))
        normed[rows, :] = (block.astype(F32) - centre) * scale

    @pl.when(first)
    def _():
        load_x[0].wait()
        low[c], centre, scale = normalise(xin[c].astype(F32))
        keep_stats(slice(None), xin[c, :, window], centre, scale)

    def to_core(slot, replica):
        block = wp.at[my_rows, cols_of(replica)]
        one = copier(slot, block, block, core)
        one.start()
        sent.append(one)

    from_y = [zh * 4 + (y + 4 - j) % 4 for j in (1, 2, 3)]
    from_zy = [(1 - zh) * 4 + (y + 4 - j) % 4 for j in (1, 2, 3)]
    for j in range(3):
        arrived(W_Y + j, wp.at[my_rows, cols_of(from_y[j])])
        to_core(W_C + 2 + j, from_y[j])

    @pl.when(second)
    def _():
        pl.semaphore_wait(go, 1)
        for one in w_far:
            one.start()

    for t in range(2):
        held = wp.at[my_cuts[t], cols_of(other)]
        arrived(W_Z + t, held)
        for j in range(3):
            one = copier(W_ZY + 3 * t + j, held, held, ys[j])
            one.start()
            sent.append(one)

    @pl.when(first)
    def _():
        pl.semaphore_signal(go, inc=1, device_id=across, device_id_type=pl.DeviceIdType.MESH)

    to_core(W_C + 1, other)
    for j in range(3):
        for t in range(2):
            arrived(W_ZY + 3 * t + j, wp.at[my_cuts[t], cols_of(from_zy[j])])
        to_core(W_C + 5 + j, from_zy[j])
    for i, replica in enumerate([dp, other] + from_y + from_zy):
        arrived(W_C + i, wp.at[core_rows, cols_of(replica)])

    def column_sums():
        csum[...] = lax.dot_general(
            jnp.ones((16, D), BF16), wp[...], (((1,), (1,)), ((), ())), preferred_element_type=F32
        )

    own = [xg.at[x, zq, rows] for rows in pieces]
    x_up = [copier(X_UP + t, xout.at[pieces[t]], own[t], across) for t in range(2)]
    x_z = [copier(X_Z + 3 * t + j, own[t], own[t], zs[j]) for t in range(2) for j in range(3)]
    x_x = []
    for t in range(2):
        for i in range(4):
            block = xg.at[x, (zq + 4 - i) % 4, pieces[t]]
            x_x += [copier(X_X + 12 * t + 3 * i + j, block, block, xs[j]) for j in range(3)]
    swap_low = copier(LOW, low.at[c], low.at[c], core)
    b_x = []
    for t in range(2):
        for i in range(4):
            q = (zq + 1 + i) % 4
            for j in range(3):
                block = bsend.at[(x + 1 + j) % 4, q, pieces[t]]
                landing = brecv.at[j, q, pieces[t]]
                b_x.append(copier(B_X + 12 * t + 3 * i + j, block, landing, xs[j]))

    @pl.when(second)
    def _():
        column_sums()
        for t in range(2):
            arrived(X_UP + t, own[t])
            for one in x_z[3 * t : 3 * t + 3] + x_x[12 * t : 12 * t + 3]:
                one.start()
        for t in range(2):
            for j in range(3):
                arrived(X_Z + 3 * t + j, xg.at[x, (zq + 3 - j) % 4, pieces[t]])
                for one in x_x[12 * t + 3 * j + 3 : 12 * t + 3 * j + 6]:
                    one.start()
        load_cot.wait()

    def gathered(t):
        for i in range(4):
            for j in range(3):
                block = xg.at[(x + 3 - j) % 4, (zq + 4 - i) % 4, pieces[t]]
                arrived(X_X + 12 * t + 3 * i + j, block)
        rows = pieces[t]
        left = lax.broadcasted_iota(jnp.int32, (PIECE, 128), 1) < 64
        parts = []
        for m in range(8):
            even = xg[m % 2 * 2, m // 2, rows].astype(F32)
            late = xg[m % 2 * 2 + 1, m // 2, rows].astype(F32)
            middle = jnp.where(left, even[:, 128:], late[:, :128])
            parts += [even[:, :128], middle, late[:, 128:]]
        low[c, rows], centre, scale = normalise(jnp.concatenate(parts, axis=1))
        keep_stats(rows, xg[x, zq, rows], centre, scale)

    def find_slope(rows, upstream):
        up[rows, :] = upstream.astype(F32)
        slopes[rows, :] = (up[rows, :] * slope_of[rows, :]).astype(BF16)

    def back(rows, size, messages):
        slope = slopes[rows, :]
        wide = slope.astype(F32)
        r1 = jnp.sum(wide * csum[0:1, :], axis=1, keepdims=True) * (SCALE / D)
        r2 = jnp.sum(wide * mixed[rows, :], axis=1, keepdims=True) * (1.0 / D)
        h1 = r1.astype(BF16).astype(F32)
        h2 = r2.astype(BF16).astype(F32)
        lane = lax.broadcasted_iota(jnp.int32, (size, 128), 1)
        spot = lane % 64
        sums = jnp.where(
            spot == 0, h1, jnp.where(spot == 1, r1 - h1, jnp.where(spot == 2, h2, r2 - h2))
        )
        for i in range(4):
            q = (zq + 1 + i) % 4
            for half in range(2):
                cols = pl.ds(pl.multiple_of(q * 768 + half * 384, 384), 384)
                part = SCALE * jnp.dot(slope, wp[:, cols], preferred_element_type=F32)
                middle = part[:, 128:256]
                even = jnp.concatenate([part[:, :128], jnp.where(lane < 64, middle, sums)], axis=1)
                late = jnp.concatenate([jnp.where(lane < 64, sums, middle), part[:, 256:]], axis=1)
                bsend[2 * half, q, rows] = even.astype(BF16)
                bsend[2 * half + 1, q, rows] = late.astype(BF16)
            for one in messages[3 * i : 3 * i + 3] + messages[3 * i + 12 : 3 * i + 15]:
                one.start()

    for t in range(2):
        rows = pieces[t]

        @pl.when(second)
        def _():
            gathered(t)

        z = SCALE * lax.dot_general(
            low[c, rows], wp[...], (((1,), (1,)), ((), ())), preferred_element_type=F32
        )
        value, slope_value = gelu_both(z)
        mixed[rows, :] = z
        slope_of[rows, :] = slope_value

        @pl.when(first)
        def _():
            xout[rows, :] = (xin[c, rows, window].astype(F32) + value).astype(BF16)
            x_up[t].start()

        @pl.when(second)
        def _():
            find_slope(rows, cot[rows, :])
            back(rows, PIECE, b_x[12 * t : 12 * t + 12])
            x2_w[rows, :] = (xg[x, zq, rows].astype(F32) + value).astype(BF16)

    @pl.when(first)
    def _():
        load_x[1].wait()
        low[1 - c], _, _ = normalise(xin[1 - c].astype(F32))
        column_sums()
        for t in range(2):
            arrived(G_DOWN + t, g_in.at[pieces[t]])
            find_slope(pieces[t], g_in[pieces[t], :])

    swap_slope = copier(SLOPE, slope_t.at[core_rows], sl.at[c], core)
    slope_t[...] = slopes[...].T
    swap_slope.start()
    sl[c] = slope_t[my_rows, :]
    swap_x2 = copier(X2, x2_t.at[core_rows], x2.at[c], core)

    @pl.when(second)
    def _():
        swap_low.start()
        x2_t[...] = x2_w[...].T
        swap_x2.start()
        x2[c] = x2_t[my_rows, :]
        arrived(LOW, low.at[1 - c])

    arrived(SLOPE, sl.at[1 - c])
    whole = jnp.concatenate([sl[0], sl[1]], axis=1)
    g_y = []
    for i, half in enumerate((1 - zh, zh)):
        for j in range(4):
            to = (y + 1 + j) % 4
            cols = cols_of(half * 4 + to)
            rows = low[:, :, cols].reshape(2 * HALF, ROWS)
            part = jnp.dot(whole, rows, preferred_element_type=F32)
            gsend[half, to] = (part * SCALE).astype(BF16)
            if j < 3:
                if i == 0:
                    some = [
                        copier(G_YO + 2 * j + t, gsend.at[half, to, cuts[t]], grecv.at[i, j, cuts[t]], ys[j])
                        for t in range(2)
                    ]
                else:
                    some = [copier(G_YS + j, gsend.at[half, to], grecv.at[i, j], ys[j])]
                for one in some:
                    one.start()
                g_y += some

    send_far = [copier(G_Z + t, gzs.at[cuts[t]], gzr.at[cuts[t]], far) for t in range(2)]

    def reduce_far():
        for t in range(2):
            total = gsend[1 - zh, y, cuts[t]].astype(F32)
            for j in range(3):
                arrived(G_YO + 2 * j + t, grecv.at[0, j, cuts[t]])
                total = total + grecv[0, j, cuts[t]].astype(F32)
            gzs[cuts[t], :] = total.astype(BF16)
            send_far[t].start()

    @pl.when(first)
    def _():
        back(slice(None), HALF, b_x)
        reduce_far()

    b_z = []
    for t in range(2):
        rows = pieces[t]
        for i in range(4):
            q = (zq + 1 + i) % 4
            total = bsend[x, q, rows].astype(F32)
            for j in range(3):
                arrived(B_X + 12 * t + 3 * i + j, brecv.at[j, q, rows])
                total = total + brecv[j, q, rows].astype(F32)
            if i < 3:
                zsend[q, rows] = total.astype(BF16)
                one = copier(B_Z + 3 * t + i, zsend.at[q, rows], zrecv.at[i, rows], zs[i])
                one.start()
                b_z.append(one)
            else:
                zacc[rows, :] = total

    g_down = [copier(G_DOWN + t, gout.at[pieces[t]], g_in.at[pieces[t]], across) for t in range(2)]
    for t in range(2):
        rows = pieces[t]
        total = zacc[rows, :]
        for j in range(3):
            arrived(B_Z + 3 * t + j, zrecv.at[j, rows])
            total = total + zrecv[j, rows].astype(F32)
        tail = jnp.where(odd == 0, total[:, PAIR:], total[:, : WIDE - PAIR])
        r1 = tail[:, 0:1] + tail[:, 1:2]
        r2 = tail[:, 2:3] + tail[:, 3:4]
        change = inv[rows, 0:1] * (total - r1 - normed[rows, :] * r2)
        gout[rows, :] = (up[rows, :] + change).astype(BF16)

        @pl.when(second)
        def _():
            g_down[t].start()

    @pl.when(second)
    def _():
        reduce_far()

    g_t[...] = gout[...].T
    swap_g = copier(G_C, g_t.at[core_rows], gc.at[c], core)
    swap_g.start()
    gc[c] = g_t[my_rows, :]

    send_spare = copier(SPARE, x2, spare_in, across)

    @pl.when(second)
    def _():
        arrived(X2, x2.at[1 - c])
        send_spare.start()

    total = gsend[zh, y].astype(F32)
    for j in range(3):
        arrived(G_YS + j, grecv.at[1, j])
        total = total + grecv[1, j].astype(F32)
    load_m1.wait()
    load_m2.wait()
    for t in range(2):
        arrived(G_Z + t, gzr.at[cuts[t]])
    gradient = total + gzr[...].astype(F32)
    moment1 = 0.9 * m1v[...] + 0.1 * gradient
    moment2 = 0.95 * m2v[...] + 0.05 * gradient * gradient
    update = moment1 / FIRST_FIX / (jnp.sqrt(moment2 / SECOND_FIX) + 1e-08)
    plain = wv[...].astype(F32)
    stepped = (plain - 0.05 * (update + 0.1 * plain)).astype(BF16)
    copy_out[...] = stepped
    send_copy = copier(COPY, copy_out, copy_in, across)

    @pl.when(second)
    def _():
        send_copy.start()
        spare[...] = jnp.zeros_like(spare)
        copy[...] = jnp.zeros_like(copy)

    new_m1[...] = moment1
    new_m2[...] = moment2
    new_w[...] = stepped

    arrived(G_C, gc.at[1 - c])
    grad[...] = jnp.concatenate([gc[0], gc[1]], axis=1)

    @pl.when(first)
    def _():
        arrived(SPARE, spare_in)
        spare[...] = jnp.concatenate([spare_in[0], spare_in[1]], axis=1)
        arrived(COPY, copy_in)
        copy[...] = copy_in[...]
        for one in x_up:
            one.wait_send()

    for one in sent + [swap_slope, swap_g] + send_far + b_x + b_z + g_y:
        one.wait_send()

    @pl.when(second)
    def _():
        for one in x_z + x_x + g_down + [swap_low, swap_x2, send_spare, send_copy]:
            one.wait_send()


def per_device(inputs, cotangent, weight, moment1, moment2):
    vmem = pl.BlockSpec(memory_space=pltpu.VMEM)
    anywhere = pl.BlockSpec(memory_space=pl.ANY)
    shape = jax.ShapeDtypeStruct
    outs = [
        shape((LANE, 2 * HALF), BF16),
        shape((LANE, 2 * HALF), BF16),
        shape((LANE, ROWS), BF16),
        shape((LANE, ROWS), F32),
        shape((LANE, ROWS), F32),
        shape((LANE, ROWS), BF16),
    ]
    scratch = [
        ((2, HALF, D), BF16),
        ((HALF, WIDE), BF16),
        ((LANE, ROWS), BF16),
        ((LANE, ROWS), F32),
        ((LANE, ROWS), F32),
        ((WIDE, D), BF16),
        ((16, WIDE), F32),
        ((2, HALF, D), BF16),
        ((4, 4, HALF, WIDE), BF16),
        ((HALF, WIDE), BF16),
        ((HALF, WIDE), F32),
        ((HALF, 128), F32),
        ((HALF, WIDE), F32),
        ((HALF, WIDE), F32),
        ((HALF, WIDE), F32),
        ((HALF, WIDE), BF16),
        ((WIDE, HALF), BF16),
        ((2, LANE, HALF), BF16),
        ((WIDE, HALF), BF16),
        ((2, LANE, HALF), BF16),
        ((2, LANE, HALF), BF16),
        ((4, 4, HALF, WIDE), BF16),
        ((3, 4, HALF, WIDE), BF16),
        ((HALF, WIDE), F32),
        ((4, HALF, WIDE), BF16),
        ((3, HALF, WIDE), BF16),
        ((HALF, WIDE), BF16),
        ((WIDE, HALF), BF16),
        ((2, LANE, HALF), BF16),
        ((2, 4, LANE, ROWS), BF16),
        ((2, 3, LANE, ROWS), BF16),
        ((LANE, ROWS), BF16),
        ((LANE, ROWS), BF16),
        ((LANE, ROWS), BF16),
        ((LANE, ROWS), BF16),
        ((HALF, WIDE), BF16),
        ((HALF, WIDE), BF16),
    ]
    results = pl.pallas_call(
        kernel,
        out_shape=outs,
        in_specs=[anywhere] * 5,
        out_specs=[vmem] * 6,
        scratch_shapes=[pltpu.VMEM(dims, kind) for dims, kind in scratch]
        + [pltpu.SemaphoreType.DMA((SLOTS,))] * 2
        + [pltpu.SemaphoreType.DMA((6,)), pltpu.SemaphoreType.REGULAR],
        compiler_params=pltpu.CompilerParams(
            collective_id=0, has_side_effects=True, vmem_limit_bytes=53 * 2**20
        ),
    )(inputs, cotangent, weight.T, moment1.T, moment2.T)
    return tuple(one.T for one in results)


def solution(mesh):
    split = P("dp", "section")
    return jax.shard_map(
        per_device,
        mesh=mesh,
        in_specs=(P("dp", None), P("dp", None), split, split, split),
        out_specs=(split,) * 6,
        check_vma=False,
    )
```

time: 107 us -> 102 us (0.953)
  Pallas kernels: 97.1 us -> 94.3 us
  local copies, waits for them, and re-layouts: 8.76 us -> 6.5 us
    pallas_call x1, Pallas kernels: 97.1 us -> 94.3 us  [per_device(): pl.pallas_call(kernel, out_shape=outs, in_specs=[anywhere] * 5, out_specs...]
    unnamed x16 -> x12, local copies, waits for them, and re-layouts: 8.76 us -> 6.5 us
where the time goes in v2:
time: 102 us; the launch traced here: 101 us
  Pallas kernels  94.3 us (92%)
  local copies, waits for them, and re-layouts  6.5 us (6%)
    pallas_call x1, Pallas kernels, per_device(): pl.pallas_call(kernel, out_shape=outs, in_specs=[anywhere] * 5, out_specs...  94.3 us
    unnamed x12, local copies, waits for them, and re-layouts  6.5 us

profile of v2, /device:TPU:1, one launch (start us, length us, event | category | flops | bytes accessed | tf_op | source)
XLA Modules:
  0.0 101.5 jit_solution(2902879291006300058)
XLA Ops:
  0.6 0.0 copy-start
  0.6 0.9 copy-done
  1.5 0.0 copy-start.1
  1.5 0.9 copy-done.1
  2.5 0.0 copy-start.2
  2.5 0.9 copy-done.2
  3.3 94.3 %shard_map.100 = (bf16[96,128]{1,0:T(8,128)(2,1)S(1)}, bf16[96,128]{1,0:T(8,128)(2,1)S(1)}, bf16[96,384]{1,0:T(8,128)(2,1)S(1)}, f32[96,384]{1,0:T(8,128)S(1)}, ...) custom-call(bf16[128,3072]{1,0:T(8,128)(2,1)} %inputs.1, bf16[128,3072]{1,0:T(8,128)(2,1)} %cotangent.1, ...), custom_call_target="tpu_custom_call" | custom-call | tf_op jit(solution)/shard_map/pallas_call | solution.py:509
  97.6 0.6 copy.17
  98.3 0.6 copy.18
  98.9 0.6 copy.19
  99.5 0.7 copy.20
  100.2 0.7 copy.21
  100.8 0.6 copy.22
Async XLA Ops:
  0.6 0.9 copy-start
  1.5 0.9 copy-start.1
  2.5 0.9 copy-start.2

commit v3 on v2

--- a/solution.py
+++ b/solution.py
@@ -22,15 +22,16 @@
 BF16 = jnp.bfloat16
 
 PIECE = HALF // 2
-CUT = LANE // 2
-
-W_Z, W_Y, W_ZY, W_C = 0, 2, 5, 11
-X_UP, X_Z, X_X = 19, 21, 27
-LOW, X2, SPARE, SLOPE = 51, 52, 53, 54
-B_X, B_Z = 55, 79
-G_DOWN, G_C = 85, 87
-G_YO, G_YS, G_Z, COPY = 88, 94, 97, 99
-SLOTS = 100
+PACK = 48
+CUT = LANE // 3
+
+W_Z, W_Y, W_ZY, W_C = 0, 3, 6, 15
+X_UP, X_Z, X_X = 23, 25, 31
+LOW, X2, SPARE, SLOPE = 63, 64, 65, 66
+B_X, B_Z, R_X, R_Z = 67, 99, 105, 108
+G_DOWN, G_C = 111, 113
+G_YO, G_YS, G_Z, COPY = 114, 123, 126, 129
+SLOTS = 130
 
 
 def gelu_both(z):
@@ -42,8 +43,8 @@
     inputs, cotangent, w, m1, m2,
     spare, grad, new_w, new_m1, new_m2, copy,
     xin, cot, wv, m1v, m2v, wp, csum, low, xg, xout, normed, inv, mixed, slope_of, up, g_in,
-    slope_t, sl, x2_t, x2, spare_in, bsend, brecv, zacc, zsend, zrecv,
-    gout, g_t, gc, gsend, grecv, gzs, gzr, copy_out, copy_in, slopes, x2_w,
+    slope_t, sl, x2_t, x2, spare_in, bsend, halves, brecv, zacc, zsend, zrecv,
+    rsend, rrecv, rzsend, rzrecv, gpack, gout, g_t, gc, gsend, grecv, gzs, gzr, copy_out, copy_in, slopes, x2_w,
     send_sem, recv_sem, here_sem, go,
 ):
     sec = lax.axis_index("section")
@@ -115,10 +116,10 @@
     pl.semaphore_wait(barrier, len(peers))
 
     pieces = [pl.ds(PIECE * t, PIECE) for t in range(2)]
-    cuts = [pl.ds(CUT * t, CUT) for t in range(2)]
-    my_cuts = [pl.ds(pl.multiple_of(odd * 64 + c * LANE + CUT * t, 16), CUT) for t in range(2)]
-
-    w_far = [copier(W_Z + t, wv.at[cuts[t]], wp.at[my_cuts[t], cols_of(dp)], far) for t in range(2)]
+    cuts = [pl.ds(CUT * t, CUT) for t in range(3)]
+    my_cuts = [pl.ds(pl.multiple_of(odd * 64 + c * LANE + CUT * t, 32), CUT) for t in range(3)]
+
+    w_far = [copier(W_Z + t, wv.at[cuts[t]], wp.at[my_cuts[t], cols_of(dp)], far) for t in range(3)]
     mine = wp.at[my_rows, cols_of(dp)]
     sent = [copier(W_Y + j, wv, mine, ys[j]) for j in range(3)]
     sent.append(copier(W_C, wv, mine, core))
@@ -169,7 +170,7 @@
         for one in w_far:
             one.start()
 
-    for t in range(2):
+    for t in range(3):
         held = wp.at[my_cuts[t], cols_of(other)]
         arrived(W_Z + t, held)
         for j in range(3):
@@ -183,7 +184,7 @@
 
     to_core(W_C + 1, other)
     for j in range(3):
-        for t in range(2):
+        for t in range(3):
             arrived(W_ZY + 3 * t + j, wp.at[my_cuts[t], cols_of(from_zy[j])])
         to_core(W_C + 5 + j, from_zy[j])
     for i, replica in enumerate([dp, other] + from_y + from_zy):
@@ -194,82 +195,141 @@
             jnp.ones((16, D), BF16), wp[...], (((1,), (1,)), ((), ())), preferred_element_type=F32
         )
 
-    own = [xg.at[x, zq, rows] for rows in pieces]
-    x_up = [copier(X_UP + t, xout.at[pieces[t]], own[t], across) for t in range(2)]
+    left = lax.broadcasted_iota(jnp.int32, (PIECE, 128), 1) < 64
+    left16 = lax.broadcasted_iota(jnp.int32, (16, 128), 1) < 64
+
+    def turn(block):
+        return pltpu.roll(block, 64, 1)
+
+    def pack(full, shared, shift):
+        turned = turn(shared)
+        near, away = (turned, shared) if shift else (shared, turned)
+        return jnp.concatenate([full, jnp.where(left16, near[:16], away[16:])], axis=0)
+
+    def pack_own(wide):
+        low_form = pack(wide[:, :128], wide[:, 128:], False)
+        return jnp.where(odd == 0, low_form, pack(wide[:, 128:], wide[:, :128], True))
+
+    def shared_part(packed, shift):
+        end = packed[PIECE:]
+        turned = turn(end)
+        return jnp.concatenate([turned, end] if shift else [end, turned], axis=0)
+
+    def unpack_own(packed):
+        full = packed[:PIECE]
+        low_form = jnp.concatenate([full, shared_part(packed, False)], axis=1)
+        high_form = jnp.concatenate([shared_part(packed, True), full], axis=1)
+        return jnp.where(odd == 0, low_form, high_form)
+
+    upward = [pl.ds(0, 16 if i % 2 == 0 else 32) for i in range(4)]
+    downward = [pl.ds(16, 32) if i % 2 == 0 else pl.ds(32, 16) for i in range(4)]
+    ways = [(upward, xs[0]), (downward, xs[2])]
+
+    own = [xg.at[x, zq, t] for t in range(2)]
+    x_up = [copier(X_UP + t, xout.at[t], own[t], across) for t in range(2)]
     x_z = [copier(X_Z + 3 * t + j, own[t], own[t], zs[j]) for t in range(2) for j in range(3)]
-    x_x = []
+    x_x = {}
     for t in range(2):
         for i in range(4):
-            block = xg.at[x, (zq + 4 - i) % 4, pieces[t]]
-            x_x += [copier(X_X + 12 * t + 3 * i + j, block, block, xs[j]) for j in range(3)]
+            q = (zq + 4 - i) % 4
+            for way in range(2):
+                slot = X_X + 16 * t + 4 * i + way
+                block = xg.at[x, q, t]
+                x_x[t, i, way] = copier(slot, block, block, ways[way][1])
+                part = xg.at[(x + 3 + 2 * way) % 4, q, t, ways[way][0][i]]
+                x_x[t, i, way + 2] = copier(slot + 2, part, part, ways[way][1])
     swap_low = copier(LOW, low.at[c], low.at[c], core)
-    b_x = []
+
+    @pl.when(second)
+    def _():
+        column_sums()
+        for t in range(2):
+            arrived(X_UP + t, own[t])
+            for one in x_z[3 * t : 3 * t + 3] + [x_x[t, 0, 0], x_x[t, 0, 1]]:
+                one.start()
+        for t in range(2):
+            for j in range(3):
+                arrived(X_Z + 3 * t + j, xg.at[x, (zq + 3 - j) % 4, t])
+                x_x[t, j + 1, 0].start()
+                x_x[t, j + 1, 1].start()
+        load_cot.wait()
+        for t in range(2):
+            for i in range(4):
+                for way in range(2):
+                    block = xg.at[(x + 3 + 2 * way) % 4, (zq + 4 - i) % 4, t]
+                    arrived(X_X + 16 * t + 4 * i + way, block)
+                    x_x[t, i, way + 2].start()
+
+    def gathered(t):
+        for i in range(4):
+            for way in range(2):
+                block = xg.at[(x + 2) % 4, (zq + 4 - i) % 4, t, ways[way][0][i]]
+                arrived(X_X + 16 * t + 4 * i + way + 2, block)
+        rows = pieces[t]
+        parts = []
+        for m in range(8):
+            even = xg[m % 2 * 2, m // 2, t].astype(F32)
+            late = xg[m % 2 * 2 + 1, m // 2, t].astype(F32)
+            middle = jnp.where(left, shared_part(even, False), shared_part(late, True))
+            parts += [even[:PIECE], middle, late[:PIECE]]
+        low[c, rows], centre, scale = normalise(jnp.concatenate(parts, axis=1))
+        keep_stats(rows, unpack_own(xg[x, zq, t].astype(F32)), centre, scale)
+
+    def find_slope(rows, upstream):
+        up[rows, :] = upstream.astype(F32)
+        slopes[rows, :] = (up[rows, :] * slope_of[rows, :]).astype(BF16)
+
+    b_x = {}
     for t in range(2):
         for i in range(4):
             q = (zq + 1 + i) % 4
-            for j in range(3):
-                block = bsend.at[(x + 1 + j) % 4, q, pieces[t]]
-                landing = brecv.at[j, q, pieces[t]]
-                b_x.append(copier(B_X + 12 * t + 3 * i + j, block, landing, xs[j]))
-
-    @pl.when(second)
-    def _():
-        column_sums()
-        for t in range(2):
-            arrived(X_UP + t, own[t])
-            for one in x_z[3 * t : 3 * t + 3] + x_x[12 * t : 12 * t + 3]:
-                one.start()
-        for t in range(2):
-            for j in range(3):
-                arrived(X_Z + 3 * t + j, xg.at[x, (zq + 3 - j) % 4, pieces[t]])
-                for one in x_x[12 * t + 3 * j + 3 : 12 * t + 3 * j + 6]:
-                    one.start()
-        load_cot.wait()
-
-    def gathered(t):
-        for i in range(4):
-            for j in range(3):
-                block = xg.at[(x + 3 - j) % 4, (zq + 4 - i) % 4, pieces[t]]
-                arrived(X_X + 12 * t + 3 * i + j, block)
-        rows = pieces[t]
-        left = lax.broadcasted_iota(jnp.int32, (PIECE, 128), 1) < 64
-        parts = []
-        for m in range(8):
-            even = xg[m % 2 * 2, m // 2, rows].astype(F32)
-            late = xg[m % 2 * 2 + 1, m // 2, rows].astype(F32)
-            middle = jnp.where(left, even[:, 128:], late[:, :128])
-            parts += [even[:, :128], middle, late[:, 128:]]
-        low[c, rows], centre, scale = normalise(jnp.concatenate(parts, axis=1))
-        keep_stats(rows, xg[x, zq, rows], centre, scale)
-
-    def find_slope(rows, upstream):
-        up[rows, :] = upstream.astype(F32)
-        slopes[rows, :] = (up[rows, :] * slope_of[rows, :]).astype(BF16)
-
-    def back(rows, size, messages):
-        slope = slopes[rows, :]
-        wide = slope.astype(F32)
-        r1 = jnp.sum(wide * csum[0:1, :], axis=1, keepdims=True) * (SCALE / D)
-        r2 = jnp.sum(wide * mixed[rows, :], axis=1, keepdims=True) * (1.0 / D)
-        h1 = r1.astype(BF16).astype(F32)
-        h2 = r2.astype(BF16).astype(F32)
-        lane = lax.broadcasted_iota(jnp.int32, (size, 128), 1)
-        spot = lane % 64
-        sums = jnp.where(
-            spot == 0, h1, jnp.where(spot == 1, r1 - h1, jnp.where(spot == 2, h2, r2 - h2))
-        )
+            for way in range(2):
+                slot = B_X + 16 * t + 4 * i + way
+                rows, to = ways[way][0][i], ways[way][1]
+                opposite = bsend.at[(x + 2) % 4, q, t, rows]
+                b_x[t, i, way] = copier(slot, opposite, halves.at[way, q, t, rows], to)
+                block = bsend.at[(x + 1 + 2 * way) % 4, q, t]
+                b_x[t, i, way + 2] = copier(slot + 2, block, brecv.at[way, q, t], to)
+
+    def back(t):
+        slope = slopes[pieces[t], :]
         for i in range(4):
             q = (zq + 1 + i) % 4
             for half in range(2):
                 cols = pl.ds(pl.multiple_of(q * 768 + half * 384, 384), 384)
                 part = SCALE * jnp.dot(slope, wp[:, cols], preferred_element_type=F32)
                 middle = part[:, 128:256]
-                even = jnp.concatenate([part[:, :128], jnp.where(lane < 64, middle, sums)], axis=1)
-                late = jnp.concatenate([jnp.where(lane < 64, sums, middle), part[:, 256:]], axis=1)
-                bsend[2 * half, q, rows] = even.astype(BF16)
-                bsend[2 * half + 1, q, rows] = late.astype(BF16)
-            for one in messages[3 * i : 3 * i + 3] + messages[3 * i + 12 : 3 * i + 15]:
-                one.start()
+                bsend[2 * half, q, t] = pack(part[:, :128], middle, False).astype(BF16)
+                bsend[2 * half + 1, q, t] = pack(part[:, 256:], middle, True).astype(BF16)
+            b_x[t, i, 0].start()
+            b_x[t, i, 1].start()
+
+    r_x = [copier(R_X + j, rsend, rrecv.at[j], xs[j]) for j in range(3)]
+    r_z = [copier(R_Z + j, rzsend, rzrecv.at[j], zs[j]) for j in range(3)]
+
+    def give_sums():
+        wide = slopes[...].astype(F32)
+        r1 = jnp.sum(wide * csum[0:1, :], axis=1, keepdims=True) * (SCALE / D)
+        r2 = jnp.sum(wide * mixed[...], axis=1, keepdims=True) * (1.0 / D)
+        spot = lax.broadcasted_iota(jnp.int32, (HALF, 128), 1)
+        both = jnp.where(spot == 0, r1, jnp.where(spot == 1, r2, 0.0))
+        both = jnp.concatenate([both, jnp.zeros((128 - HALF, 128), F32)], axis=0)
+        rsend[...] = both.T[:8, :]
+        for one in r_x:
+            one.start()
+
+    def pass_terms():
+        for t in range(2):
+            for i in range(4):
+                q = (zq + 1 + i) % 4
+                for way in range(2):
+                    rows = ways[way][0][i]
+                    to = (x + 1 + 2 * way) % 4
+                    arrived(B_X + 16 * t + 4 * i + way, halves.at[way, q, t, rows])
+                    mine = bsend[to, q, t, rows].astype(F32)
+                    mine = mine + halves[way, q, t, rows].astype(F32)
+                    bsend[to, q, t, rows] = mine.astype(BF16)
+                    b_x[t, i, way + 2].start()
 
     for t in range(2):
         rows = pieces[t]
@@ -287,14 +347,14 @@
 
         @pl.when(first)
         def _():
-            xout[rows, :] = (xin[c, rows, window].astype(F32) + value).astype(BF16)
+            xout[t] = pack_own(xin[c, rows, window].astype(F32) + value).astype(BF16)
             x_up[t].start()
 
         @pl.when(second)
         def _():
             find_slope(rows, cot[rows, :])
-            back(rows, PIECE, b_x[12 * t : 12 * t + 12])
-            x2_w[rows, :] = (xg[x, zq, rows].astype(F32) + value).astype(BF16)
+            back(t)
+            x2_w[rows, :] = (unpack_own(xg[x, zq, t].astype(F32)) + value).astype(BF16)
 
     @pl.when(first)
     def _():
@@ -302,8 +362,8 @@
         low[1 - c], _, _ = normalise(xin[1 - c].astype(F32))
         column_sums()
         for t in range(2):
-            arrived(G_DOWN + t, g_in.at[pieces[t]])
-            find_slope(pieces[t], g_in[pieces[t], :])
+            arrived(G_DOWN + t, g_in.at[t])
+            find_slope(pieces[t], unpack_own(g_in[t].astype(F32)))
 
     swap_slope = copier(SLOPE, slope_t.at[core_rows], sl.at[c], core)
     slope_t[...] = slopes[...].T
@@ -313,6 +373,8 @@
 
     @pl.when(second)
     def _():
+        give_sums()
+        pass_terms()
         swap_low.start()
         x2_t[...] = x2_w[...].T
         swap_x2.start()
@@ -332,8 +394,13 @@
             if j < 3:
                 if i == 0:
                     some = [
-                        copier(G_YO + 2 * j + t, gsend.at[half, to, cuts[t]], grecv.at[i, j, cuts[t]], ys[j])
-                        for t in range(2)
+                        copier(
+                            G_YO + 3 * j + t,
+                            gsend.at[half, to, cuts[t]],
+                            grecv.at[i, j, cuts[t]],
+                            ys[j],
+                        )
+                        for t in range(3)
                     ]
                 else:
                     some = [copier(G_YS + j, gsend.at[half, to], grecv.at[i, j], ys[j])]
@@ -341,54 +408,70 @@
                     one.start()
                 g_y += some
 
-    send_far = [copier(G_Z + t, gzs.at[cuts[t]], gzr.at[cuts[t]], far) for t in range(2)]
+    send_far = [copier(G_Z + t, gzs.at[cuts[t]], gzr.at[cuts[t]], far) for t in range(3)]
 
     def reduce_far():
-        for t in range(2):
+        for t in range(3):
             total = gsend[1 - zh, y, cuts[t]].astype(F32)
             for j in range(3):
-                arrived(G_YO + 2 * j + t, grecv.at[0, j, cuts[t]])
+                arrived(G_YO + 3 * j + t, grecv.at[0, j, cuts[t]])
                 total = total + grecv[0, j, cuts[t]].astype(F32)
             gzs[cuts[t], :] = total.astype(BF16)
             send_far[t].start()
 
     @pl.when(first)
     def _():
-        back(slice(None), HALF, b_x)
+        back(0)
+        back(1)
+        give_sums()
         reduce_far()
+        pass_terms()
 
     b_z = []
     for t in range(2):
-        rows = pieces[t]
         for i in range(4):
             q = (zq + 1 + i) % 4
-            total = bsend[x, q, rows].astype(F32)
-            for j in range(3):
-                arrived(B_X + 12 * t + 3 * i + j, brecv.at[j, q, rows])
-                total = total + brecv[j, q, rows].astype(F32)
+            total = bsend[x, q, t].astype(F32)
+            for way in range(2):
+                arrived(B_X + 16 * t + 4 * i + way + 2, brecv.at[way, q, t])
+                total = total + brecv[way, q, t].astype(F32)
             if i < 3:
-                zsend[q, rows] = total.astype(BF16)
-                one = copier(B_Z + 3 * t + i, zsend.at[q, rows], zrecv.at[i, rows], zs[i])
+                zsend[q, t] = total.astype(BF16)
+                one = copier(B_Z + 3 * t + i, zsend.at[q, t], zrecv.at[i, t], zs[i])
                 one.start()
                 b_z.append(one)
             else:
-                zacc[rows, :] = total
-
-    g_down = [copier(G_DOWN + t, gout.at[pieces[t]], g_in.at[pieces[t]], across) for t in range(2)]
+                zacc[t] = total
+        if t == 0:
+            sums = rsend[...]
+            for j in range(3):
+                arrived(R_X + j, rrecv.at[j])
+                sums = sums + rrecv[j]
+            rzsend[...] = sums
+            for one in r_z:
+                one.start()
+
+    sums = rzsend[...]
+    for j in range(3):
+        arrived(R_Z + j, rzrecv.at[j])
+        sums = sums + rzrecv[j]
+    sums = jnp.concatenate([sums, jnp.zeros((120, 128), F32)], axis=0).T
+    g_down = [copier(G_DOWN + t, gpack.at[t], g_in.at[t], across) for t in range(2)]
     for t in range(2):
         rows = pieces[t]
-        total = zacc[rows, :]
+        total = zacc[t]
         for j in range(3):
-            arrived(B_Z + 3 * t + j, zrecv.at[j, rows])
-            total = total + zrecv[j, rows].astype(F32)
-        tail = jnp.where(odd == 0, total[:, PAIR:], total[:, : WIDE - PAIR])
-        r1 = tail[:, 0:1] + tail[:, 1:2]
-        r2 = tail[:, 2:3] + tail[:, 3:4]
-        change = inv[rows, 0:1] * (total - r1 - normed[rows, :] * r2)
-        gout[rows, :] = (up[rows, :] + change).astype(BF16)
+            arrived(B_Z + 3 * t + j, zrecv.at[j, t])
+            total = total + zrecv[j, t].astype(F32)
+        r1 = sums[PIECE * t : PIECE * t + PIECE, 0:1]
+        r2 = sums[PIECE * t : PIECE * t + PIECE, 1:2]
+        change = inv[rows, 0:1] * (unpack_own(total) - r1 - normed[rows, :] * r2)
+        renewed = up[rows, :] + change
+        gout[rows, :] = renewed.astype(BF16)
 
         @pl.when(second)
         def _():
+            gpack[t] = pack_own(renewed).astype(BF16)
             g_down[t].start()
 
     @pl.when(second)
@@ -413,7 +496,7 @@
         total = total + grecv[1, j].astype(F32)
     load_m1.wait()
     load_m2.wait()
-    for t in range(2):
+    for t in range(3):
         arrived(G_Z + t, gzr.at[cuts[t]])
     gradient = total + gzr[...].astype(F32)
     moment1 = 0.9 * m1v[...] + 0.1 * gradient
@@ -446,12 +529,12 @@
         for one in x_up:
             one.wait_send()
 
-    for one in sent + [swap_slope, swap_g] + send_far + b_x + b_z + g_y:
+    for one in sent + [swap_slope, swap_g] + send_far + list(b_x.values()) + b_z + g_y + r_x + r_z:
         one.wait_send()
 
     @pl.when(second)
     def _():
-        for one in x_z + x_x + g_down + [swap_low, swap_x2, send_spare, send_copy]:
+        for one in x_z + list(x_x.values()) + g_down + [swap_low, swap_x2, send_spare, send_copy]:
             one.wait_send()
 
 
@@ -476,24 +559,30 @@
         ((WIDE, D), BF16),
         ((16, WIDE), F32),
         ((2, HALF, D), BF16),
-        ((4, 4, HALF, WIDE), BF16),
-        ((HALF, WIDE), BF16),
+        ((4, 4, 2, PACK, 128), BF16),
+        ((2, PACK, 128), BF16),
         ((HALF, WIDE), F32),
         ((HALF, 128), F32),
         ((HALF, WIDE), F32),
         ((HALF, WIDE), F32),
         ((HALF, WIDE), F32),
-        ((HALF, WIDE), BF16),
+        ((2, PACK, 128), BF16),
         ((WIDE, HALF), BF16),
         ((2, LANE, HALF), BF16),
         ((WIDE, HALF), BF16),
         ((2, LANE, HALF), BF16),
         ((2, LANE, HALF), BF16),
-        ((4, 4, HALF, WIDE), BF16),
-        ((3, 4, HALF, WIDE), BF16),
-        ((HALF, WIDE), F32),
-        ((4, HALF, WIDE), BF16),
-        ((3, HALF, WIDE), BF16),
+        ((4, 4, 2, PACK, 128), BF16),
+        ((2, 4, 2, PACK, 128), BF16),
+        ((2, 4, 2, PACK, 128), BF16),
+        ((2, PACK, 128), F32),
+        ((4, 2, PACK, 128), BF16),
+        ((3, 2, PACK, 128), BF16),
+        ((8, 128), F32),
+        ((3, 8, 128), F32),
+        ((8, 128), F32),
+        ((3, 8, 128), F32),
+        ((2, PACK, 128), BF16),
         ((HALF, WIDE), BF16),
         ((WIDE, HALF), BF16),
         ((2, LANE, HALF), BF16),
@@ -515,7 +604,7 @@
         + [pltpu.SemaphoreType.DMA((SLOTS,))] * 2
         + [pltpu.SemaphoreType.DMA((6,)), pltpu.SemaphoreType.REGULAR],
         compiler_params=pltpu.CompilerParams(
-            collective_id=0, has_side_effects=True, vmem_limit_bytes=53 * 2**20
+            collective_id=0, has_side_effects=True, vmem_limit_bytes=54656 * 2**10
         ),
     )(inputs, cotangent, weight.T, moment1.T, moment2.T)
     return tuple(one.T for one in results)

time: 102 us -> 105 us (1.029)
  Pallas kernels: 94.3 us -> 99.1 us
  local copies, waits for them, and re-layouts: 6.5 us -> 4.68 us
    pallas_call x1, Pallas kernels: 94.3 us -> 99.1 us  [per_device(): pl.pallas_call(kernel, out_shape=outs, in_specs=[anywhere] * 5, out_specs...]
    unnamed x12 -> x8, local copies, waits for them, and re-layouts: 6.5 us -> 4.68 us
where the time goes in v3:
time: 105 us; the launch traced here: 104 us
  Pallas kernels  99.1 us (94%)
  local copies, waits for them, and re-layouts  4.68 us (4%)
    pallas_call x1, Pallas kernels, per_device(): pl.pallas_call(kernel, out_shape=outs, in_specs=[anywhere] * 5, out_specs...  99.1 us
    unnamed x8, local copies, waits for them, and re-layouts  4.68 us

profile of v3, /device:TPU:1, one launch (start us, length us, event | category | flops | bytes accessed | tf_op | source)
XLA Modules:
  0.0 104.4 jit_solution(10665473153063936109)
XLA Ops:
  0.6 0.0 copy-start
  0.6 0.9 copy-done
  1.5 99.1 %shard_map.100 = (bf16[96,128]{1,0:T(8,128)(2,1)S(1)}, bf16[96,128]{1,0:T(8,128)(2,1)S(1)}, bf16[96,384]{1,0:T(8,128)(2,1)S(1)}, f32[96,384]{1,0:T(8,128)S(1)}, ...) custom-call(bf16[128,3072]{1,0:T(8,128)(2,1)} %inputs.1, bf16[128,3072]{1,0:T(8,128)(2,1)} %cotangent.1, ...), custom_call_target="tpu_custom_call" | custom-call | tf_op jit(solution)/shard_map/pallas_call | solution.py:598
  100.6 0.6 copy.17
  101.2 0.6 copy.18
  101.8 0.6 copy.19
  102.5 0.7 copy.20
  103.1 0.7 copy.21
  103.8 0.6 copy.22
Async XLA Ops:
  0.6 0.9 copy-start

commit v4 on v3

--- a/solution.py
+++ b/solution.py
@@ -27,11 +27,12 @@
 
 W_Z, W_Y, W_ZY, W_C = 0, 3, 6, 15
 X_UP, X_Z, X_X = 23, 25, 31
-LOW, X2, SPARE, SLOPE = 63, 64, 65, 66
-B_X, B_Z, R_X, R_Z = 67, 99, 105, 108
-G_DOWN, G_C = 111, 113
-G_YO, G_YS, G_Z, COPY = 114, 123, 126, 129
-SLOTS = 130
+LOW, X2, SPARE, SLOPE = 55, 56, 57, 58
+B_X, B_Z, R_X, R_Z = 59, 83, 89, 92
+G_DOWN, G_C = 95, 97
+G_YO, G_YS, G_Z, COPY = 98, 107, 110, 113
+S_Y, L_Y = 114, 121
+SLOTS = 127
 
 
 def gelu_both(z):
@@ -43,8 +44,9 @@
     inputs, cotangent, w, m1, m2,
     spare, grad, new_w, new_m1, new_m2, copy,
     xin, cot, wv, m1v, m2v, wp, csum, low, xg, xout, normed, inv, mixed, slope_of, up, g_in,
-    slope_t, sl, x2_t, x2, spare_in, bsend, halves, brecv, zacc, zsend, zrecv,
+    slope_t, sl, x2_t, x2, spare_in, bsend, brecv, zacc, zsend, zrecv,
     rsend, rrecv, rzsend, rzrecv, gpack, gout, g_t, gc, gsend, grecv, gzs, gzr, copy_out, copy_in, slopes, x2_w,
+    spack, sg, lowx, gown,
     send_sem, recv_sem, here_sem, go,
 ):
     sec = lax.axis_index("section")
@@ -109,7 +111,8 @@
     load_m2.start()
 
     barrier = pltpu.get_barrier_semaphore()
-    peers = [core, across, far] + ys + xs + zs
+    ys_core = [{"section": core["section"], "dp": one["dp"]} for one in ys]
+    peers = [core, across, far] + ys + ys_core + xs + zs
     for peer in peers:
         pl.semaphore_signal(barrier, inc=1, device_id=peer, device_id_type=pl.DeviceIdType.MESH)
     load_w.wait()
@@ -221,23 +224,15 @@
         high_form = jnp.concatenate([shared_part(packed, True), full], axis=1)
         return jnp.where(odd == 0, low_form, high_form)
 
-    upward = [pl.ds(0, 16 if i % 2 == 0 else 32) for i in range(4)]
-    downward = [pl.ds(16, 32) if i % 2 == 0 else pl.ds(32, 16) for i in range(4)]
-    ways = [(upward, xs[0]), (downward, xs[2])]
-
     own = [xg.at[x, zq, t] for t in range(2)]
     x_up = [copier(X_UP + t, xout.at[t], own[t], across) for t in range(2)]
     x_z = [copier(X_Z + 3 * t + j, own[t], own[t], zs[j]) for t in range(2) for j in range(3)]
     x_x = {}
     for t in range(2):
         for i in range(4):
-            q = (zq + 4 - i) % 4
-            for way in range(2):
-                slot = X_X + 16 * t + 4 * i + way
-                block = xg.at[x, q, t]
-                x_x[t, i, way] = copier(slot, block, block, ways[way][1])
-                part = xg.at[(x + 3 + 2 * way) % 4, q, t, ways[way][0][i]]
-                x_x[t, i, way + 2] = copier(slot + 2, part, part, ways[way][1])
+            block = xg.at[x, (zq + 4 - i) % 4, t]
+            for j in range(3):
+                x_x[t, i, j] = copier(X_X + 12 * t + 3 * i + j, block, block, xs[j])
     swap_low = copier(LOW, low.at[c], low.at[c], core)
 
     @pl.when(second)
@@ -245,26 +240,20 @@
         column_sums()
         for t in range(2):
             arrived(X_UP + t, own[t])
-            for one in x_z[3 * t : 3 * t + 3] + [x_x[t, 0, 0], x_x[t, 0, 1]]:
+            for one in x_z[3 * t : 3 * t + 3] + [x_x[t, 0, j] for j in range(3)]:
                 one.start()
         for t in range(2):
             for j in range(3):
                 arrived(X_Z + 3 * t + j, xg.at[x, (zq + 3 - j) % 4, t])
-                x_x[t, j + 1, 0].start()
-                x_x[t, j + 1, 1].start()
+                for k in range(3):
+                    x_x[t, j + 1, k].start()
         load_cot.wait()
-        for t in range(2):
-            for i in range(4):
-                for way in range(2):
-                    block = xg.at[(x + 3 + 2 * way) % 4, (zq + 4 - i) % 4, t]
-                    arrived(X_X + 16 * t + 4 * i + way, block)
-                    x_x[t, i, way + 2].start()
 
     def gathered(t):
         for i in range(4):
-            for way in range(2):
-                block = xg.at[(x + 2) % 4, (zq + 4 - i) % 4, t, ways[way][0][i]]
-                arrived(X_X + 16 * t + 4 * i + way + 2, block)
+            for j in range(3):
+                block = xg.at[(x + 3 - j) % 4, (zq + 4 - i) % 4, t]
+                arrived(X_X + 12 * t + 3 * i + j, block)
         rows = pieces[t]
         parts = []
         for m in range(8):
@@ -283,13 +272,9 @@
     for t in range(2):
         for i in range(4):
             q = (zq + 1 + i) % 4
-            for way in range(2):
-                slot = B_X + 16 * t + 4 * i + way
-                rows, to = ways[way][0][i], ways[way][1]
-                opposite = bsend.at[(x + 2) % 4, q, t, rows]
-                b_x[t, i, way] = copier(slot, opposite, halves.at[way, q, t, rows], to)
-                block = bsend.at[(x + 1 + 2 * way) % 4, q, t]
-                b_x[t, i, way + 2] = copier(slot + 2, block, brecv.at[way, q, t], to)
+            for j in range(3):
+                block = bsend.at[(x + 1 + j) % 4, q, t]
+                b_x[t, i, j] = copier(B_X + 12 * t + 3 * i + j, block, brecv.at[j, q, t], xs[j])
 
     def back(t):
         slope = slopes[pieces[t], :]
@@ -301,8 +286,8 @@
                 middle = part[:, 128:256]
                 bsend[2 * half, q, t] = pack(part[:, :128], middle, False).astype(BF16)
                 bsend[2 * half + 1, q, t] = pack(part[:, 256:], middle, True).astype(BF16)
-            b_x[t, i, 0].start()
-            b_x[t, i, 1].start()
+            for j in range(3):
+                b_x[t, i, j].start()
 
     r_x = [copier(R_X + j, rsend, rrecv.at[j], xs[j]) for j in range(3)]
     r_z = [copier(R_Z + j, rzsend, rzrecv.at[j], zs[j]) for j in range(3)]
@@ -318,18 +303,11 @@
         for one in r_x:
             one.start()
 
-    def pass_terms():
-        for t in range(2):
-            for i in range(4):
-                q = (zq + 1 + i) % 4
-                for way in range(2):
-                    rows = ways[way][0][i]
-                    to = (x + 1 + 2 * way) % 4
-                    arrived(B_X + 16 * t + 4 * i + way, halves.at[way, q, t, rows])
-                    mine = bsend[to, q, t, rows].astype(F32)
-                    mine = mine + halves[way, q, t, rows].astype(F32)
-                    bsend[to, q, t, rows] = mine.astype(BF16)
-                    b_x[t, i, way + 2].start()
+    low_y = {}
+    for i, half in enumerate((1 - zh, zh)):
+        for j in range(3):
+            cols = cols_of(half * 4 + (y + 1 + j) % 4)
+            low_y[i, j] = copier(L_Y + 3 * i + j, low.at[:, :, cols], lowx.at[i, y], ys[j])
 
     for t in range(2):
         rows = pieces[t]
@@ -360,81 +338,115 @@
     def _():
         load_x[1].wait()
         low[1 - c], _, _ = normalise(xin[1 - c].astype(F32))
+        for one in low_y.values():
+            one.start()
+        for i, half in enumerate((1 - zh, zh)):
+            lowx[i, y] = low[:, :, cols_of(half * 4 + y)]
         column_sums()
         for t in range(2):
             arrived(G_DOWN + t, g_in.at[t])
             find_slope(pieces[t], unpack_own(g_in[t].astype(F32)))
-
+            back(t)
+
+    give_sums()
+    slope_t[...] = slopes[...].T
     swap_slope = copier(SLOPE, slope_t.at[core_rows], sl.at[c], core)
-    slope_t[...] = slopes[...].T
-    swap_slope.start()
-    sl[c] = slope_t[my_rows, :]
     swap_x2 = copier(X2, x2_t.at[core_rows], x2.at[c], core)
-
-    @pl.when(second)
-    def _():
-        give_sums()
-        pass_terms()
+    send_far = [copier(G_Z + t, gzs.at[cuts[t]], gzr.at[cuts[t]], far) for t in range(3)]
+
+    def reduce_far():
+        for t in range(3):
+            total = gsend[1 - zh, y, cuts[t]].astype(F32)
+            for j in range(3):
+                arrived(G_YO + 3 * j + t, grecv.at[0, j, cuts[t]])
+                total = total + grecv[0, j, cuts[t]].astype(F32)
+            gzs[cuts[t], :] = total.astype(BF16)
+            send_far[t].start()
+
+    g_y = []
+    for i, half in enumerate((1 - zh, zh)):
+        for j in range(3):
+            to = (y + 1 + j) % 4
+            if i == 0:
+                g_y += [
+                    copier(
+                        G_YO + 3 * j + t,
+                        gsend.at[half, to, cuts[t]],
+                        grecv.at[i, j, cuts[t]],
+                        ys[j],
+                    )
+                    for t in range(3)
+                ]
+            else:
+                g_y.append(copier(G_YS + j, gsend.at[half, to], grecv.at[i, j], ys[j]))
+
+    @pl.when(second)
+    def _():
+        swap_slope.start()
+        sl[c] = slope_t[my_rows, :]
         swap_low.start()
         x2_t[...] = x2_w[...].T
         swap_x2.start()
         x2[c] = x2_t[my_rows, :]
         arrived(LOW, low.at[1 - c])
-
-    arrived(SLOPE, sl.at[1 - c])
-    whole = jnp.concatenate([sl[0], sl[1]], axis=1)
-    g_y = []
-    for i, half in enumerate((1 - zh, zh)):
-        for j in range(4):
-            to = (y + 1 + j) % 4
-            cols = cols_of(half * 4 + to)
-            rows = low[:, :, cols].reshape(2 * HALF, ROWS)
-            part = jnp.dot(whole, rows, preferred_element_type=F32)
-            gsend[half, to] = (part * SCALE).astype(BF16)
-            if j < 3:
-                if i == 0:
-                    some = [
-                        copier(
-                            G_YO + 3 * j + t,
-                            gsend.at[half, to, cuts[t]],
-                            grecv.at[i, j, cuts[t]],
-                            ys[j],
-                        )
-                        for t in range(3)
-                    ]
-                else:
-                    some = [copier(G_YS + j, gsend.at[half, to], grecv.at[i, j], ys[j])]
-                for one in some:
-                    one.start()
-                g_y += some
-
-    send_far = [copier(G_Z + t, gzs.at[cuts[t]], gzr.at[cuts[t]], far) for t in range(3)]
-
-    def reduce_far():
-        for t in range(3):
-            total = gsend[1 - zh, y, cuts[t]].astype(F32)
-            for j in range(3):
-                arrived(G_YO + 3 * j + t, grecv.at[0, j, cuts[t]])
-                total = total + grecv[0, j, cuts[t]].astype(F32)
-            gzs[cuts[t], :] = total.astype(BF16)
-            send_far[t].start()
+        arrived(SLOPE, sl.at[1 - c])
+        whole = jnp.concatenate([sl[0], sl[1]], axis=1)
+        for i, half in enumerate((1 - zh, zh)):
+            for j in range(4):
+                to = (y + 1 + j) % 4
+                rows = low[:, :, cols_of(half * 4 + to)].reshape(2 * HALF, ROWS)
+                part = jnp.dot(whole, rows, preferred_element_type=F32)
+                gsend[half, to] = (part * SCALE).astype(BF16)
+                if j < 3:
+                    for one in g_y[3 * j : 3 * j + 3] if i == 0 else g_y[9 + j : 10 + j]:
+                        one.start()
+
+    s_y = {}
+    for flip in range(2):
+        for dy in range(4):
+            if flip + dy:
+                to = core if dy == 0 else (ys_core if flip else ys)[dy - 1]
+                s_y[flip, dy] = copier(S_Y + 2 * dy + flip - 1, spack.at[flip], sg.at[y, c], to)
 
     @pl.when(first)
     def _():
-        back(0)
-        back(1)
-        give_sums()
-        reduce_far()
-        pass_terms()
+        for flip, rows in enumerate((my_rows, core_rows)):
+            block = slope_t[rows, :]
+            spack[flip] = jnp.concatenate([block[:48], block[48:]], axis=1)
+        for one in s_y.values():
+            one.start()
+        sg[y, c] = spack[0]
+        for i in range(2):
+            for j in range(3):
+                arrived(L_Y + 3 * i + j, lowx.at[i, (y + 3 - j) % 4])
+        for dy in range(4):
+            for flip in range(2):
+                if flip + dy:
+                    block = sg.at[(y + 4 - dy) % 4, c + flip - 2 * c * flip]
+                    arrived(S_Y + 2 * dy + flip - 1, block)
+        left48 = lax.broadcasted_iota(jnp.int32, (PACK, 128), 1) < 64
+        parts = []
+        for k in range(4):
+            even, late = sg[k, 0].astype(F32), sg[k, 1].astype(F32)
+            upper = jnp.where(left48, even, turn(late))
+            lower = jnp.where(left48, turn(even), late)
+            parts.append(jnp.concatenate([upper, lower], axis=0).astype(BF16))
+        whole = jnp.concatenate(parts, axis=1)
+        part = jnp.dot(whole, lowx[0].reshape(8 * HALF, ROWS), preferred_element_type=F32)
+        gzs[...] = (part * SCALE).astype(BF16)
+        for one in send_far:
+            one.start()
+        part = jnp.dot(whole, lowx[1].reshape(8 * HALF, ROWS), preferred_element_type=F32)
+        gown[...] = part * SCALE
 
     b_z = []
     for t in range(2):
         for i in range(4):
             q = (zq + 1 + i) % 4
             total = bsend[x, q, t].astype(F32)
-            for way in range(2):
-                arrived(B_X + 16 * t + 4 * i + way + 2, brecv.at[way, q, t])
-                total = total + brecv[way, q, t].astype(F32)
+            for j in range(3):
+                arrived(B_X + 12 * t + 3 * i + j, brecv.at[j, q, t])
+                total = total + brecv[j, q, t].astype(F32)
             if i < 3:
                 zsend[q, t] = total.astype(BF16)
                 one = copier(B_Z + 3 * t + i, zsend.at[q, t], zrecv.at[i, t], zs[i])
@@ -490,15 +502,42 @@
         arrived(X2, x2.at[1 - c])
         send_spare.start()
 
-    total = gsend[zh, y].astype(F32)
-    for j in range(3):
-        arrived(G_YS + j, grecv.at[1, j])
-        total = total + grecv[1, j].astype(F32)
+        total = gsend[zh, y].astype(F32)
+        for j in range(3):
+            arrived(G_YS + j, grecv.at[1, j])
+            total = total + grecv[1, j].astype(F32)
+        gown[...] = total
+        spare[...] = jnp.zeros_like(spare)
+        copy[...] = jnp.zeros_like(copy)
+
+    @pl.when(first)
+    def _():
+        arrived(SPARE, spare_in)
+        spare[...] = jnp.concatenate([spare_in[0], spare_in[1]], axis=1)
+        arrived(COPY, copy_in)
+        copy[...] = copy_in[...]
+        for one in x_up + list(low_y.values()) + list(s_y.values()):
+            one.wait_send()
+
+    for one in sent + list(b_x.values()) + b_z + r_x + r_z:
+        one.wait_send()
+
+    @pl.when(second)
+    def _():
+        for one in x_z + list(x_x.values()) + g_down + g_y:
+            one.wait_send()
+        for one in (swap_slope, swap_low, swap_x2, send_spare):
+            one.wait_send()
+
+    arrived(G_C, gc.at[1 - c])
+    grad[...] = jnp.concatenate([gc[0], gc[1]], axis=1)
+    swap_g.wait_send()
+
     load_m1.wait()
     load_m2.wait()
     for t in range(3):
         arrived(G_Z + t, gzr.at[cuts[t]])
-    gradient = total + gzr[...].astype(F32)
+    gradient = gown[...] + gzr[...].astype(F32)
     moment1 = 0.9 * m1v[...] + 0.1 * gradient
     moment2 = 0.95 * m2v[...] + 0.05 * gradient * gradient
     update = moment1 / FIRST_FIX / (jnp.sqrt(moment2 / SECOND_FIX) + 1e-08)
@@ -510,32 +549,16 @@
     @pl.when(second)
     def _():
         send_copy.start()
-        spare[...] = jnp.zeros_like(spare)
-        copy[...] = jnp.zeros_like(copy)
 
     new_m1[...] = moment1
     new_m2[...] = moment2
     new_w[...] = stepped
-
-    arrived(G_C, gc.at[1 - c])
-    grad[...] = jnp.concatenate([gc[0], gc[1]], axis=1)
-
-    @pl.when(first)
-    def _():
-        arrived(SPARE, spare_in)
-        spare[...] = jnp.concatenate([spare_in[0], spare_in[1]], axis=1)
-        arrived(COPY, copy_in)
-        copy[...] = copy_in[...]
-        for one in x_up:
-            one.wait_send()
-
-    for one in sent + [swap_slope, swap_g] + send_far + list(b_x.values()) + b_z + g_y + r_x + r_z:
+    for one in send_far:
         one.wait_send()
 
     @pl.when(second)
     def _():
-        for one in x_z + list(x_x.values()) + g_down + [swap_low, swap_x2, send_spare, send_copy]:
-            one.wait_send()
+        send_copy.wait_send()
 
 
 def per_device(inputs, cotangent, weight, moment1, moment2):
@@ -573,8 +596,7 @@
         ((2, LANE, HALF), BF16),
         ((2, LANE, HALF), BF16),
         ((4, 4, 2, PACK, 128), BF16),
-        ((2, 4, 2, PACK, 128), BF16),
-        ((2, 4, 2, PACK, 128), BF16),
+        ((3, 4, 2, PACK, 128), BF16),
         ((2, PACK, 128), F32),
         ((4, 2, PACK, 128), BF16),
         ((3, 2, PACK, 128), BF16),
@@ -594,6 +616,10 @@
         ((LANE, ROWS), BF16),
         ((HALF, WIDE), BF16),
         ((HALF, WIDE), BF16),
+        ((2, PACK, 128), BF16),
+        ((4, 2, PACK, 128), BF16),
+        ((2, 4, 2, HALF, ROWS), BF16),
+        ((LANE, ROWS), F32),
     ]
     results = pl.pallas_call(
         kernel,

time: 105 us -> 97.6 us (0.930)
  Pallas kernels: 99.1 us -> 91 us
    pallas_call x1, Pallas kernels: 99.1 us -> 91 us  [per_device(): pl.pallas_call(kernel, out_shape=outs, in_specs=[anywhere] * 5, out_specs...]
where the time goes in v4:
time: 97.6 us; the launch traced here: 96.3 us
  Pallas kernels  91 us (93%)
  local copies, waits for them, and re-layouts  4.68 us (5%)
    pallas_call x1, Pallas kernels, per_device(): pl.pallas_call(kernel, out_shape=outs, in_specs=[anywhere] * 5, out_specs...  91 us
    unnamed x8, local copies, waits for them, and re-layouts  4.68 us

profile of v4, /device:TPU:1, one launch (start us, length us, event | category | flops | bytes accessed | tf_op | source)
XLA Modules:
  0.0 96.3 jit_solution(9474739875467645274)
XLA Ops:
  0.6 0.0 copy-start
  0.6 0.9 copy-done
  1.5 91.0 %shard_map.100 = (bf16[96,128]{1,0:T(8,128)(2,1)S(1)}, bf16[96,128]{1,0:T(8,128)(2,1)S(1)}, bf16[96,384]{1,0:T(8,128)(2,1)S(1)}, f32[96,384]{1,0:T(8,128)S(1)}, ...) custom-call(bf16[128,3072]{1,0:T(8,128)(2,1)} %inputs.1, bf16[128,3072]{1,0:T(8,128)(2,1)} %cotangent.1, ...), custom_call_target="tpu_custom_call" | custom-call | tf_op jit(solution)/shard_map/pallas_call | solution.py:624
  92.5 0.6 copy.17
  93.2 0.6 copy.18
  93.8 0.6 copy.19
  94.4 0.7 copy.20
  95.1 0.7 copy.21
  95.7 0.6 copy.22
Async XLA Ops:
  0.6 0.9 copy-start

commit v5 on v4

--- a/solution.py
+++ b/solution.py
@@ -40,14 +40,22 @@
     return z * cdf, cdf + z * jnp.exp(-0.5 * z * z) * 0.3989422804014327
 
 
+def stepped(weight, moment1, moment2, gradient):
+    moment1 = 0.9 * moment1 + 0.1 * gradient
+    moment2 = 0.95 * moment2 + 0.05 * gradient * gradient
+    update = moment1 / FIRST_FIX / (jnp.sqrt(moment2 / SECOND_FIX) + 1e-08)
+    plain = weight.astype(F32)
+    return (plain - 0.05 * (update + 0.1 * plain)).astype(BF16), moment1, moment2
+
+
 def kernel(
     inputs, cotangent, w, m1, m2,
-    spare, grad, new_w, new_m1, new_m2, copy,
+    spare, grad, gradient, copy,
     xin, cot, wv, m1v, m2v, wp, csum, low, xg, xout, normed, inv, mixed, slope_of, up, g_in,
     slope_t, sl, x2_t, x2, spare_in, bsend, brecv, zacc, zsend, zrecv,
     rsend, rrecv, rzsend, rzrecv, gpack, gout, g_t, gc, gsend, grecv, gzs, gzr, copy_out, copy_in, slopes, x2_w,
     spack, sg, lowx, gown,
-    send_sem, recv_sem, here_sem, go,
+    send_sem, recv_sem, here_sem,
 ):
     sec = lax.axis_index("section")
     dp = lax.axis_index("dp")
@@ -106,9 +114,8 @@
     @pl.when(second)
     def _():
         load_cot.start()
-
-    load_m1.start()
-    load_m2.start()
+        load_m1.start()
+        load_m2.start()
 
     barrier = pltpu.get_barrier_semaphore()
     ys_core = [{"section": core["section"], "dp": one["dp"]} for one in ys]
@@ -169,7 +176,6 @@
 
     @pl.when(second)
     def _():
-        pl.semaphore_wait(go, 1)
         for one in w_far:
             one.start()
 
@@ -181,17 +187,30 @@
             one.start()
             sent.append(one)
 
-    @pl.when(first)
-    def _():
-        pl.semaphore_signal(go, inc=1, device_id=across, device_id_type=pl.DeviceIdType.MESH)
+    near = pl.ds(pl.multiple_of(zh * 1536, 1536), 1536)
+    away = pl.ds(pl.multiple_of((1 - zh) * 1536, 1536), 1536)
+
+    def times_weight(rows, cols):
+        return SCALE * lax.dot_general(
+            low[c, rows, cols], wp[:, cols], (((1,), (1,)), ((), ())), preferred_element_type=F32
+        )
+
+    @pl.when(first)
+    def _():
+        for i, replica in zip((0, 2, 3, 4), [dp] + from_y):
+            arrived(W_C + i, wp.at[core_rows, cols_of(replica)])
+        mixed[...] = times_weight(slice(None), near)
 
     to_core(W_C + 1, other)
     for j in range(3):
         for t in range(3):
             arrived(W_ZY + 3 * t + j, wp.at[my_cuts[t], cols_of(from_zy[j])])
         to_core(W_C + 5 + j, from_zy[j])
-    for i, replica in enumerate([dp, other] + from_y + from_zy):
-        arrived(W_C + i, wp.at[core_rows, cols_of(replica)])
+
+    @pl.when(first)
+    def _():
+        for i, replica in zip((1, 5, 6, 7), [other] + from_zy):
+            arrived(W_C + i, wp.at[core_rows, cols_of(replica)])
 
     def column_sums():
         csum[...] = lax.dot_general(
@@ -237,7 +256,6 @@
 
     @pl.when(second)
     def _():
-        column_sums()
         for t in range(2):
             arrived(X_UP + t, own[t])
             for one in x_z[3 * t : 3 * t + 3] + [x_x[t, 0, j] for j in range(3)]:
@@ -247,6 +265,9 @@
                 arrived(X_Z + 3 * t + j, xg.at[x, (zq + 3 - j) % 4, t])
                 for k in range(3):
                     x_x[t, j + 1, k].start()
+        for i, replica in enumerate([dp, other] + from_y + from_zy):
+            arrived(W_C + i, wp.at[core_rows, cols_of(replica)])
+        column_sums()
         load_cot.wait()
 
     def gathered(t):
@@ -315,12 +336,15 @@
         @pl.when(second)
         def _():
             gathered(t)
-
-        z = SCALE * lax.dot_general(
-            low[c, rows], wp[...], (((1,), (1,)), ((), ())), preferred_element_type=F32
-        )
-        value, slope_value = gelu_both(z)
-        mixed[rows, :] = z
+            mixed[rows, :] = times_weight(rows, slice(None))
+            if t == 1:
+                swap_low.start()
+
+        @pl.when(first)
+        def _():
+            mixed[rows, :] = mixed[rows, :] + times_weight(rows, away)
+
+        value, slope_value = gelu_both(mixed[rows, :])
         slope_of[rows, :] = slope_value
 
         @pl.when(first)
@@ -362,6 +386,54 @@
                 total = total + grecv[0, j, cuts[t]].astype(F32)
             gzs[cuts[t], :] = total.astype(BF16)
             send_far[t].start()
+
+    b_z = []
+
+    def sum_terms(t):
+        for i in range(4):
+            q = (zq + 1 + i) % 4
+            total = bsend[x, q, t].astype(F32)
+            for j in range(3):
+                arrived(B_X + 12 * t + 3 * i + j, brecv.at[j, q, t])
+                total = total + brecv[j, q, t].astype(F32)
+            if i < 3:
+                zsend[q, t] = total.astype(BF16)
+                one = copier(B_Z + 3 * t + i, zsend.at[q, t], zrecv.at[i, t], zs[i])
+                one.start()
+                b_z.append(one)
+            else:
+                zacc[t] = total
+        if t == 0:
+            sums = rsend[...]
+            for j in range(3):
+                arrived(R_X + j, rrecv.at[j])
+                sums = sums + rrecv[j]
+            rzsend[...] = sums
+            for one in r_z:
+                one.start()
+
+    s_y = {}
+    for flip in range(2):
+        for dy in range(4):
+            if flip + dy:
+                to = core if dy == 0 else (ys_core if flip else ys)[dy - 1]
+                s_y[flip, dy] = copier(S_Y + 2 * dy + flip - 1, spack.at[flip], sg.at[y, c], to)
+
+    @pl.when(second)
+    def _():
+        swap_slope.start()
+        sl[c] = slope_t[my_rows, :]
+
+    @pl.when(first)
+    def _():
+        for flip, rows in enumerate((my_rows, core_rows)):
+            block = slope_t[rows, :]
+            spack[flip] = jnp.concatenate([block[:48], block[48:]], axis=1)
+        for one in s_y.values():
+            one.start()
+        sg[y, c] = spack[0]
+
+    sum_terms(0)
 
     g_y = []
     for i, half in enumerate((1 - zh, zh)):
@@ -382,12 +454,6 @@
 
     @pl.when(second)
     def _():
-        swap_slope.start()
-        sl[c] = slope_t[my_rows, :]
-        swap_low.start()
-        x2_t[...] = x2_w[...].T
-        swap_x2.start()
-        x2[c] = x2_t[my_rows, :]
         arrived(LOW, low.at[1 - c])
         arrived(SLOPE, sl.at[1 - c])
         whole = jnp.concatenate([sl[0], sl[1]], axis=1)
@@ -401,21 +467,8 @@
                     for one in g_y[3 * j : 3 * j + 3] if i == 0 else g_y[9 + j : 10 + j]:
                         one.start()
 
-    s_y = {}
-    for flip in range(2):
-        for dy in range(4):
-            if flip + dy:
-                to = core if dy == 0 else (ys_core if flip else ys)[dy - 1]
-                s_y[flip, dy] = copier(S_Y + 2 * dy + flip - 1, spack.at[flip], sg.at[y, c], to)
-
-    @pl.when(first)
-    def _():
-        for flip, rows in enumerate((my_rows, core_rows)):
-            block = slope_t[rows, :]
-            spack[flip] = jnp.concatenate([block[:48], block[48:]], axis=1)
-        for one in s_y.values():
-            one.start()
-        sg[y, c] = spack[0]
+    @pl.when(first)
+    def _():
         for i in range(2):
             for j in range(3):
                 arrived(L_Y + 3 * i + j, lowx.at[i, (y + 3 - j) % 4])
@@ -439,29 +492,7 @@
         part = jnp.dot(whole, lowx[1].reshape(8 * HALF, ROWS), preferred_element_type=F32)
         gown[...] = part * SCALE
 
-    b_z = []
-    for t in range(2):
-        for i in range(4):
-            q = (zq + 1 + i) % 4
-            total = bsend[x, q, t].astype(F32)
-            for j in range(3):
-                arrived(B_X + 12 * t + 3 * i + j, brecv.at[j, q, t])
-                total = total + brecv[j, q, t].astype(F32)
-            if i < 3:
-                zsend[q, t] = total.astype(BF16)
-                one = copier(B_Z + 3 * t + i, zsend.at[q, t], zrecv.at[i, t], zs[i])
-                one.start()
-                b_z.append(one)
-            else:
-                zacc[t] = total
-        if t == 0:
-            sums = rsend[...]
-            for j in range(3):
-                arrived(R_X + j, rrecv.at[j])
-                sums = sums + rrecv[j]
-            rzsend[...] = sums
-            for one in r_z:
-                one.start()
+    sum_terms(1)
 
     sums = rzsend[...]
     for j in range(3):
@@ -499,6 +530,9 @@
 
     @pl.when(second)
     def _():
+        x2_t[...] = x2_w[...].T
+        swap_x2.start()
+        x2[c] = x2_t[my_rows, :]
         arrived(X2, x2.at[1 - c])
         send_spare.start()
 
@@ -533,26 +567,19 @@
     grad[...] = jnp.concatenate([gc[0], gc[1]], axis=1)
     swap_g.wait_send()
 
-    load_m1.wait()
-    load_m2.wait()
     for t in range(3):
         arrived(G_Z + t, gzr.at[cuts[t]])
-    gradient = gown[...] + gzr[...].astype(F32)
-    moment1 = 0.9 * m1v[...] + 0.1 * gradient
-    moment2 = 0.95 * m2v[...] + 0.05 * gradient * gradient
-    update = moment1 / FIRST_FIX / (jnp.sqrt(moment2 / SECOND_FIX) + 1e-08)
-    plain = wv[...].astype(F32)
-    stepped = (plain - 0.05 * (update + 0.1 * plain)).astype(BF16)
-    copy_out[...] = stepped
+    total = gown[...] + gzr[...].astype(F32)
+    gradient[...] = total
     send_copy = copier(COPY, copy_out, copy_in, across)
 
     @pl.when(second)
     def _():
+        load_m1.wait()
+        load_m2.wait()
+        copy_out[...] = stepped(wv[...], m1v[...], m2v[...], total)[0]
         send_copy.start()
 
-    new_m1[...] = moment1
-    new_m2[...] = moment2
-    new_w[...] = stepped
     for one in send_far:
         one.wait_send()
 
@@ -568,8 +595,6 @@
     outs = [
         shape((LANE, 2 * HALF), BF16),
         shape((LANE, 2 * HALF), BF16),
-        shape((LANE, ROWS), BF16),
-        shape((LANE, ROWS), F32),
         shape((LANE, ROWS), F32),
         shape((LANE, ROWS), BF16),
     ]
@@ -621,19 +646,20 @@
         ((2, 4, 2, HALF, ROWS), BF16),
         ((LANE, ROWS), F32),
     ]
-    results = pl.pallas_call(
+    spare, grad, gradient, copy = pl.pallas_call(
         kernel,
         out_shape=outs,
         in_specs=[anywhere] * 5,
-        out_specs=[vmem] * 6,
+        out_specs=[vmem] * 4,
         scratch_shapes=[pltpu.VMEM(dims, kind) for dims, kind in scratch]
         + [pltpu.SemaphoreType.DMA((SLOTS,))] * 2
-        + [pltpu.SemaphoreType.DMA((6,)), pltpu.SemaphoreType.REGULAR],
+        + [pltpu.SemaphoreType.DMA((6,))],
         compiler_params=pltpu.CompilerParams(
             collective_id=0, has_side_effects=True, vmem_limit_bytes=54656 * 2**10
         ),
     )(inputs, cotangent, weight.T, moment1.T, moment2.T)
-    return tuple(one.T for one in results)
+    new = stepped(weight, moment1, moment2, gradient.T)
+    return (spare.T, grad.T) + new + (copy.T,)
 
 
 def solution(mesh):

time: 97.6 us -> 91.9 us (0.942)
  Pallas kernels: 91 us -> 85.7 us
  local copies, waits for them, and re-layouts: 4.68 us -> 3.64 us
    pallas_call x1, Pallas kernels: 91 us -> 85.7 us  [per_device(): pl.pallas_call(kernel, out_shape=outs, in_specs=[anywhere] * 5, out_specs...]
    unnamed x8 -> x9, local copies, waits for them, and re-layouts: 4.68 us -> 3.64 us
where the time goes in v5:
time: 91.9 us; the launch traced here: 90.8 us
  Pallas kernels  85.7 us (93%)
  local copies, waits for them, and re-layouts  3.64 us (4%)
    pallas_call x1, Pallas kernels, per_device(): pl.pallas_call(kernel, out_shape=outs, in_specs=[anywhere] * 5, out_specs...  85.7 us
    unnamed x9, local copies, waits for them, and re-layouts  3.64 us

profile of v5, /device:TPU:1, one launch (start us, length us, event | category | flops | bytes accessed | tf_op | source)
XLA Modules:
  0.0 90.8 jit_solution(6707804424146069571)
XLA Ops:
  0.6 0.0 copy-start
  0.6 0.9 copy-done
  1.5 0.0 copy-start.1
  1.5 0.9 copy-done.1
  2.4 0.0 copy-start.2
  2.4 85.7 %shard_map.100 = (bf16[96,128]{1,0:T(8,128)(2,1)S(1)}, bf16[96,128]{1,0:T(8,128)(2,1)S(1)}, f32[96,384]{1,0:T(8,128)S(1)}, bf16[96,384]{1,0:T(8,128)(2,1)S(1)}) custom-call(bf16[128,3072]{1,0:T(8,128)(2,1)} %inputs.1, bf16[128,3072]{1,0:T(8,128)(2,1)} %cotangent.1, bf16[96,384]{1,0:T(8,128)(2,1)S(1)} %bitcast.14, f32[96,384]{1,0:T(8,128)S(1)} %bitcast.13, ...), custom_call_target="tpu_custom_call" | custom-call | tf_op jit(solution)/shard_map/pallas_call | solution.py:649
  88.2 0.0 copy-done.2
  88.2 0.8 fusion.2
  89.0 0.6 copy.14
  89.6 0.6 copy.15
  90.2 0.6 copy.16
Async XLA Ops:
  0.6 0.9 %copy-start = (f32[384,96]{0,1:T(8,128)S(1)}, f32[384,96]{0,1:T(8,128)}, u32[]{:S(2)}) copy-start(f32[384,96]{0,1:T(8,128)} %param.8) | copy-start | bytes 442372
  1.5 0.9 copy-start.1
  2.4 85.7 %copy-start.2 = (f32[384,96]{0,1:T(8,128)S(1)}, f32[384,96]{0,1:T(8,128)}, u32[]{:S(2)}) copy-start(f32[384,96]{0,1:T(8,128)} %param.9) | copy-start | bytes 442372

commit v6 on v5

--- a/solution.py
+++ b/solution.py
@@ -54,7 +54,7 @@
     xin, cot, wv, m1v, m2v, wp, csum, low, xg, xout, normed, inv, mixed, slope_of, up, g_in,
     slope_t, sl, x2_t, x2, spare_in, bsend, brecv, zacc, zsend, zrecv,
     rsend, rrecv, rzsend, rzrecv, gpack, gout, g_t, gc, gsend, grecv, gzs, gzr, copy_out, copy_in, slopes, x2_w,
-    spack, sg, lowx, gown,
+    spack, sg, lowx, gown, wide_t,
     send_sem, recv_sem, here_sem,
 ):
     sec = lax.axis_index("section")
@@ -248,33 +248,30 @@
     x_z = [copier(X_Z + 3 * t + j, own[t], own[t], zs[j]) for t in range(2) for j in range(3)]
     x_x = {}
     for t in range(2):
-        for i in range(4):
-            block = xg.at[x, (zq + 4 - i) % 4, t]
-            for j in range(3):
-                x_x[t, i, j] = copier(X_X + 12 * t + 3 * i + j, block, block, xs[j])
+        column = xg.at[x, :, t]
+        for j in range(3):
+            x_x[t, j] = copier(X_X + 3 * t + j, column, column, xs[j])
     swap_low = copier(LOW, low.at[c], low.at[c], core)
 
     @pl.when(second)
     def _():
         for t in range(2):
             arrived(X_UP + t, own[t])
-            for one in x_z[3 * t : 3 * t + 3] + [x_x[t, 0, j] for j in range(3)]:
+            for one in x_z[3 * t : 3 * t + 3]:
                 one.start()
         for t in range(2):
             for j in range(3):
                 arrived(X_Z + 3 * t + j, xg.at[x, (zq + 3 - j) % 4, t])
-                for k in range(3):
-                    x_x[t, j + 1, k].start()
+            for j in range(3):
+                x_x[t, j].start()
         for i, replica in enumerate([dp, other] + from_y + from_zy):
             arrived(W_C + i, wp.at[core_rows, cols_of(replica)])
         column_sums()
         load_cot.wait()
 
     def gathered(t):
-        for i in range(4):
-            for j in range(3):
-                block = xg.at[(x + 3 - j) % 4, (zq + 4 - i) % 4, t]
-                arrived(X_X + 12 * t + 3 * i + j, block)
+        for j in range(3):
+            arrived(X_X + 3 * t + j, xg.at[(x + 3 - j) % 4, :, t])
         rows = pieces[t]
         parts = []
         for m in range(8):
@@ -291,24 +288,21 @@
 
     b_x = {}
     for t in range(2):
-        for i in range(4):
-            q = (zq + 1 + i) % 4
-            for j in range(3):
-                block = bsend.at[(x + 1 + j) % 4, q, t]
-                b_x[t, i, j] = copier(B_X + 12 * t + 3 * i + j, block, brecv.at[j, q, t], xs[j])
+        for j in range(3):
+            column = bsend.at[(x + 1 + j) % 4, :, t]
+            b_x[t, j] = copier(B_X + 3 * t + j, column, brecv.at[j, :, t], xs[j])
 
     def back(t):
         slope = slopes[pieces[t], :]
-        for i in range(4):
-            q = (zq + 1 + i) % 4
+        for q in range(4):
             for half in range(2):
-                cols = pl.ds(pl.multiple_of(q * 768 + half * 384, 384), 384)
+                cols = pl.ds(q * 768 + half * 384, 384)
                 part = SCALE * jnp.dot(slope, wp[:, cols], preferred_element_type=F32)
                 middle = part[:, 128:256]
                 bsend[2 * half, q, t] = pack(part[:, :128], middle, False).astype(BF16)
                 bsend[2 * half + 1, q, t] = pack(part[:, 256:], middle, True).astype(BF16)
-            for j in range(3):
-                b_x[t, i, j].start()
+        for j in range(3):
+            b_x[t, j].start()
 
     r_x = [copier(R_X + j, rsend, rrecv.at[j], xs[j]) for j in range(3)]
     r_z = [copier(R_Z + j, rzsend, rzrecv.at[j], zs[j]) for j in range(3)]
@@ -390,11 +384,12 @@
     b_z = []
 
     def sum_terms(t):
+        for j in range(3):
+            arrived(B_X + 3 * t + j, brecv.at[j, :, t])
         for i in range(4):
             q = (zq + 1 + i) % 4
             total = bsend[x, q, t].astype(F32)
             for j in range(3):
-                arrived(B_X + 12 * t + 3 * i + j, brecv.at[j, q, t])
                 total = total + brecv[j, q, t].astype(F32)
             if i < 3:
                 zsend[q, t] = total.astype(BF16)
@@ -489,10 +484,14 @@
         gzs[...] = (part * SCALE).astype(BF16)
         for one in send_far:
             one.start()
-        part = jnp.dot(whole, lowx[1].reshape(8 * HALF, ROWS), preferred_element_type=F32)
-        gown[...] = part * SCALE
+        wide_t[...] = whole
 
     sum_terms(1)
+
+    @pl.when(first)
+    def _():
+        rows = lowx[1].reshape(8 * HALF, ROWS)
+        gown[...] = SCALE * jnp.dot(wide_t[...], rows, preferred_element_type=F32)
 
     sums = rzsend[...]
     for j in range(3):
@@ -645,6 +644,7 @@
         ((4, 2, PACK, 128), BF16),
         ((2, 4, 2, HALF, ROWS), BF16),
         ((LANE, ROWS), F32),
+        ((LANE, 8 * HALF), BF16),
     ]
     spare, grad, gradient, copy = pl.pallas_call(
         kernel,
@@ -655,7 +655,7 @@
         + [pltpu.SemaphoreType.DMA((SLOTS,))] * 2
         + [pltpu.SemaphoreType.DMA((6,))],
         compiler_params=pltpu.CompilerParams(
-            collective_id=0, has_side_effects=True, vmem_limit_bytes=54656 * 2**10
+            collective_id=0, has_side_effects=True, vmem_limit_bytes=54784 * 2**10
         ),
     )(inputs, cotangent, weight.T, moment1.T, moment2.T)
     new = stepped(weight, moment1, moment2, gradient.T)

time: 91.9 us -> 92.3 us (level)
  Pallas kernels: 85.7 us -> 87.9 us
    pallas_call x1, Pallas kernels: 85.7 us -> 87.9 us  [per_device(): pl.pallas_call(kernel, out_shape=outs, in_specs=[anywhere] * 5, out_specs...]
where the time goes in v6:
time: 92.3 us; the launch traced here: 92.1 us
  Pallas kernels  87.9 us (95%)
  local copies, waits for them, and re-layouts  2.73 us (3%)
    pallas_call x1, Pallas kernels, per_device(): pl.pallas_call(kernel, out_shape=outs, in_specs=[anywhere] * 5, out_specs...  87.9 us
    unnamed x9, local copies, waits for them, and re-layouts  2.73 us

profile of v6, /device:TPU:1, one launch (start us, length us, event | category | flops | bytes accessed | tf_op | source)
XLA Modules:
  0.0 92.1 jit_solution(18373252503038629110)
XLA Ops:
  0.6 0.0 copy-start
  0.6 0.9 copy-done
  1.5 0.0 copy-start.1
  1.5 0.0 copy-start.2
  1.5 87.9 %shard_map.100 = (bf16[96,128]{1,0:T(8,128)(2,1)S(1)}, bf16[96,128]{1,0:T(8,128)(2,1)S(1)}, f32[96,384]{1,0:T(8,128)S(1)}, bf16[96,384]{1,0:T(8,128)(2,1)S(1)}) custom-call(bf16[128,3072]{1,0:T(8,128)(2,1)} %inputs.1, bf16[128,3072]{1,0:T(8,128)(2,1)} %cotangent.1, bf16[96,384]{1,0:T(8,128)(2,1)S(1)} %bitcast.13, f32[96,384]{1,0:T(8,128)} %bitcast.17, ...), custom_call_target="tpu_custom_call" | custom-call | tf_op jit(solution)/shard_map/pallas_call | solution.py:649
  89.4 0.0 copy-done.1
  89.4 0.0 copy-done.2
  89.5 0.8 fusion.2
  90.3 0.6 copy.14
  90.9 0.6 copy.15
  91.5 0.6 copy.16
Async XLA Ops:
  0.6 0.9 copy-start
  1.5 87.9 %copy-start.1 = (f32[384,96]{0,1:T(8,128)S(1)}, f32[384,96]{0,1:T(8,128)}, u32[]{:S(2)}) copy-start(f32[384,96]{0,1:T(8,128)} %param.8) | copy-start | bytes 442372
  1.5 87.9 %copy-start.2 = (f32[384,96]{0,1:T(8,128)S(1)}, f32[384,96]{0,1:T(8,128)}, u32[]{:S(2)}) copy-start(f32[384,96]{0,1:T(8,128)} %param.9) | copy-start | bytes 442372

commit v7 on v5

--- a/solution.py
+++ b/solution.py
@@ -54,7 +54,7 @@
     xin, cot, wv, m1v, m2v, wp, csum, low, xg, xout, normed, inv, mixed, slope_of, up, g_in,
     slope_t, sl, x2_t, x2, spare_in, bsend, brecv, zacc, zsend, zrecv,
     rsend, rrecv, rzsend, rzrecv, gpack, gout, g_t, gc, gsend, grecv, gzs, gzr, copy_out, copy_in, slopes, x2_w,
-    spack, sg, lowx, gown,
+    spack, sg, lowx, gown, wide_t,
     send_sem, recv_sem, here_sem,
 ):
     sec = lax.axis_index("section")
@@ -433,40 +433,6 @@
             one.start()
         sg[y, c] = spack[0]
 
-    sum_terms(0)
-
-    g_y = []
-    for i, half in enumerate((1 - zh, zh)):
-        for j in range(3):
-            to = (y + 1 + j) % 4
-            if i == 0:
-                g_y += [
-                    copier(
-                        G_YO + 3 * j + t,
-                        gsend.at[half, to, cuts[t]],
-                        grecv.at[i, j, cuts[t]],
-                        ys[j],
-                    )
-                    for t in range(3)
-                ]
-            else:
-                g_y.append(copier(G_YS + j, gsend.at[half, to], grecv.at[i, j], ys[j]))
-
-    @pl.when(second)
-    def _():
-        arrived(LOW, low.at[1 - c])
-        arrived(SLOPE, sl.at[1 - c])
-        whole = jnp.concatenate([sl[0], sl[1]], axis=1)
-        for i, half in enumerate((1 - zh, zh)):
-            for j in range(4):
-                to = (y + 1 + j) % 4
-                rows = low[:, :, cols_of(half * 4 + to)].reshape(2 * HALF, ROWS)
-                part = jnp.dot(whole, rows, preferred_element_type=F32)
-                gsend[half, to] = (part * SCALE).astype(BF16)
-                if j < 3:
-                    for one in g_y[3 * j : 3 * j + 3] if i == 0 else g_y[9 + j : 10 + j]:
-                        one.start()
-
     @pl.when(first)
     def _():
         for i in range(2):
@@ -489,10 +455,48 @@
         gzs[...] = (part * SCALE).astype(BF16)
         for one in send_far:
             one.start()
-        part = jnp.dot(whole, lowx[1].reshape(8 * HALF, ROWS), preferred_element_type=F32)
-        gown[...] = part * SCALE
+        wide_t[...] = whole
+
+    sum_terms(0)
+
+    g_y = []
+    for i, half in enumerate((1 - zh, zh)):
+        for j in range(3):
+            to = (y + 1 + j) % 4
+            if i == 0:
+                g_y += [
+                    copier(
+                        G_YO + 3 * j + t,
+                        gsend.at[half, to, cuts[t]],
+                        grecv.at[i, j, cuts[t]],
+                        ys[j],
+                    )
+                    for t in range(3)
+                ]
+            else:
+                g_y.append(copier(G_YS + j, gsend.at[half, to], grecv.at[i, j], ys[j]))
+
+    @pl.when(second)
+    def _():
+        arrived(LOW, low.at[1 - c])
+        arrived(SLOPE, sl.at[1 - c])
+        whole = jnp.concatenate([sl[0], sl[1]], axis=1)
+        for i, half in enumerate((1 - zh, zh)):
+            for j in range(4):
+                to = (y + 1 + j) % 4
+                rows = low[:, :, cols_of(half * 4 + to)].reshape(2 * HALF, ROWS)
+                part = jnp.dot(whole, rows, preferred_element_type=F32)
+                gsend[half, to] = (part * SCALE).astype(BF16)
+                if j < 3:
+                    for one in g_y[3 * j : 3 * j + 3] if i == 0 else g_y[9 + j : 10 + j]:
+                        one.start()
 
     sum_terms(1)
+
+    @pl.when(first)
+    def _():
+        rows = lowx[1].reshape(8 * HALF, ROWS)
+        gown[...] = SCALE * jnp.dot(wide_t[...], rows, preferred_element_type=F32)
 
     sums = rzsend[...]
     for j in range(3):
@@ -645,6 +649,7 @@
         ((4, 2, PACK, 128), BF16),
         ((2, 4, 2, HALF, ROWS), BF16),
         ((LANE, ROWS), F32),
+        ((LANE, 8 * HALF), BF16),
     ]
     spare, grad, gradient, copy = pl.pallas_call(
         kernel,
@@ -655,7 +660,7 @@
         + [pltpu.SemaphoreType.DMA((SLOTS,))] * 2
         + [pltpu.SemaphoreType.DMA((6,))],
         compiler_params=pltpu.CompilerParams(
-            collective_id=0, has_side_effects=True, vmem_limit_bytes=54656 * 2**10
+            collective_id=0, has_side_effects=True, vmem_limit_bytes=54784 * 2**10
         ),
     )(inputs, cotangent, weight.T, moment1.T, moment2.T)
     new = stepped(weight, moment1, moment2, gradient.T)

time: 91.9 us -> 89.5 us (0.974)
  the two profiles are of different devices: /device:TPU:1 before, /device:TPU:2 now
where the time goes in v7:
time: 89.5 us; the launch traced here: 89.3 us
  Pallas kernels  85.1 us (95%)
  local copies, waits for them, and re-layouts  2.73 us (3%)
    pallas_call x1, Pallas kernels, per_device(): pl.pallas_call(kernel, out_shape=outs, in_specs=[anywhere] * 5, out_specs...  85.1 us
    unnamed x9, local copies, waits for them, and re-layouts  2.73 us

profile of v7, /device:TPU:2, one launch (start us, length us, event | category | flops | bytes accessed | tf_op | source)
XLA Modules:
  0.0 89.3 jit_solution(15795853677599354999)
XLA Ops:
  0.6 0.0 copy-start
  0.6 0.9 copy-done
  1.5 0.0 copy-start.1
  1.5 0.0 copy-start.2
  1.5 85.1 %shard_map.100 = (bf16[96,128]{1,0:T(8,128)(2,1)S(1)}, bf16[96,128]{1,0:T(8,128)(2,1)S(1)}, f32[96,384]{1,0:T(8,128)S(1)}, bf16[96,384]{1,0:T(8,128)(2,1)S(1)}) custom-call(bf16[128,3072]{1,0:T(8,128)(2,1)} %inputs.1, bf16[128,3072]{1,0:T(8,128)(2,1)} %cotangent.1, bf16[96,384]{1,0:T(8,128)(2,1)S(1)} %bitcast.13, f32[96,384]{1,0:T(8,128)} %bitcast.17, ...), custom_call_target="tpu_custom_call" | custom-call | tf_op jit(solution)/shard_map/pallas_call | solution.py:654
  86.7 0.0 copy-done.1
  86.7 0.0 copy-done.2
  86.7 0.8 fusion.2
  87.5 0.6 copy.14
  88.1 0.6 copy.15
  88.7 0.6 copy.16
Async XLA Ops:
  0.6 0.9 copy-start
  1.5 85.2 %copy-start.1 = (f32[384,96]{0,1:T(8,128)S(1)}, f32[384,96]{0,1:T(8,128)}, u32[]{:S(2)}) copy-start(f32[384,96]{0,1:T(8,128)} %param.8) | copy-start | bytes 442372
  1.5 85.2 %copy-start.2 = (f32[384,96]{0,1:T(8,128)S(1)}, f32[384,96]{0,1:T(8,128)}, u32[]{:S(2)}) copy-start(f32[384,96]{0,1:T(8,128)} %param.9) | copy-start | bytes 442372

commit v8 on v7

--- a/solution.py
+++ b/solution.py
@@ -433,8 +433,7 @@
             one.start()
         sg[y, c] = spack[0]
 
-    @pl.when(first)
-    def _():
+    def give_far():
         for i in range(2):
             for j in range(3):
                 arrived(L_Y + 3 * i + j, lowx.at[i, (y + 3 - j) % 4])
@@ -457,7 +456,17 @@
             one.start()
         wide_t[...] = whole
 
+    @pl.when(first & (zh == 1))
+    def _():
+        give_far()
+
     sum_terms(0)
+
+    sum_terms(1)
+
+    @pl.when(first & (zh == 0))
+    def _():
+        give_far()
 
     g_y = []
     for i, half in enumerate((1 - zh, zh)):
@@ -490,8 +499,6 @@
                 if j < 3:
                     for one in g_y[3 * j : 3 * j + 3] if i == 0 else g_y[9 + j : 10 + j]:
                         one.start()
-
-    sum_terms(1)
 
     @pl.when(first)
     def _():

time: 89.5 us -> 83.8 us (0.936)
  the two profiles are of different devices: /device:TPU:2 before, /device:TPU:96 now
where the time goes in v8:
time: 83.8 us; the launch traced here: 83.7 us
  Pallas kernels  79.5 us (95%)
  local copies, waits for them, and re-layouts  2.73 us (3%)
    pallas_call x1, Pallas kernels, per_device(): pl.pallas_call(kernel, out_shape=outs, in_specs=[anywhere] * 5, out_specs...  79.5 us
    unnamed x9, local copies, waits for them, and re-layouts  2.73 us

profile of v8, /device:TPU:96, one launch (start us, length us, event | category | flops | bytes accessed | tf_op | source)
XLA Modules:
  0.0 83.7 jit_solution(16615156089131475684)
XLA Ops:
  0.6 0.0 copy-start
  0.6 0.9 %copy-done = bf16[384,96]{0,1:T(8,128)(2,1)S(1)} copy-done((bf16[384,96]{0,1:T(8,128)(2,1)S(1)}, bf16[384,96]{0,1:T(8,128)(2,1)}, u32[]{:S(2)}) %copy-start) | copy-done | bytes 73752
  1.5 0.0 copy-start.1
  1.5 0.0 copy-start.2
  1.5 79.5 %shard_map.100 = (bf16[96,128]{1,0:T(8,128)(2,1)S(1)}, bf16[96,128]{1,0:T(8,128)(2,1)S(1)}, f32[96,384]{1,0:T(8,128)S(1)}, bf16[96,384]{1,0:T(8,128)(2,1)S(1)}) custom-call(bf16[128,3072]{1,0:T(8,128)(2,1)} %inputs.1, bf16[128,3072]{1,0:T(8,128)(2,1)} %cotangent.1, bf16[96,384]{1,0:T(8,128)(2,1)S(1)} %bitcast.13, f32[96,384]{1,0:T(8,128)} %bitcast.17, ...), custom_call_target="tpu_custom_call" | custom-call | tf_op jit(solution)/shard_map/pallas_call | solution.py:661
  81.0 0.0 copy-done.1
  81.0 0.0 copy-done.2
  81.0 0.8 fusion.2
  81.8 0.6 copy.14
  82.4 0.6 copy.15
  83.0 0.6 copy.16
Async XLA Ops:
  0.6 0.9 %copy-start = (bf16[384,96]{0,1:T(8,128)(2,1)S(1)}, bf16[384,96]{0,1:T(8,128)(2,1)}, u32[]{:S(2)}) copy-start(bf16[384,96]{0,1:T(8,128)(2,1)} %param.7) | copy-start | bytes 221188
  1.5 79.5 %copy-start.1 = (f32[384,96]{0,1:T(8,128)S(1)}, f32[384,96]{0,1:T(8,128)}, u32[]{:S(2)}) copy-start(f32[384,96]{0,1:T(8,128)} %param.8) | copy-start | bytes 442372
  1.5 79.5 %copy-start.2 = (f32[384,96]{0,1:T(8,128)S(1)}, f32[384,96]{0,1:T(8,128)}, u32[]{:S(2)}) copy-start(f32[384,96]{0,1:T(8,128)} %param.9) | copy-start | bytes 442372

commit v9 on v8

--- a/solution.py
+++ b/solution.py
@@ -267,7 +267,6 @@
                     x_x[t, j + 1, k].start()
         for i, replica in enumerate([dp, other] + from_y + from_zy):
             arrived(W_C + i, wp.at[core_rows, cols_of(replica)])
-        column_sums()
         load_cot.wait()
 
     def gathered(t):
@@ -371,6 +370,10 @@
             arrived(G_DOWN + t, g_in.at[t])
             find_slope(pieces[t], unpack_own(g_in[t].astype(F32)))
             back(t)
+
+    @pl.when(second)
+    def _():
+        column_sums()
 
     give_sums()
     slope_t[...] = slopes[...].T
@@ -500,11 +503,6 @@
                     for one in g_y[3 * j : 3 * j + 3] if i == 0 else g_y[9 + j : 10 + j]:
                         one.start()
 
-    @pl.when(first)
-    def _():
-        rows = lowx[1].reshape(8 * HALF, ROWS)
-        gown[...] = SCALE * jnp.dot(wide_t[...], rows, preferred_element_type=F32)
-
     sums = rzsend[...]
     for j in range(3):
         arrived(R_Z + j, rzrecv.at[j])
@@ -536,6 +534,11 @@
     swap_g = copier(G_C, g_t.at[core_rows], gc.at[c], core)
     swap_g.start()
     gc[c] = g_t[my_rows, :]
+
+    @pl.when(first)
+    def _():
+        rows = lowx[1].reshape(8 * HALF, ROWS)
+        gown[...] = SCALE * jnp.dot(wide_t[...], rows, preferred_element_type=F32)
 
     send_spare = copier(SPARE, x2, spare_in, across)
 

time: 83.8 us -> 83.5 us (level)
  no operation moved by 1% of the time
where the time goes in v9:
time: 83.5 us; the launch traced here: 83.4 us
  Pallas kernels  79.2 us (95%)
  local copies, waits for them, and re-layouts  2.73 us (3%)
    pallas_call x1, Pallas kernels, per_device(): pl.pallas_call(kernel, out_shape=outs, in_specs=[anywhere] * 5, out_specs...  79.2 us
    unnamed x9, local copies, waits for them, and re-layouts  2.73 us

profile of v9, /device:TPU:96, one launch (start us, length us, event | category | flops | bytes accessed | tf_op | source)
XLA Modules:
  0.0 83.4 jit_solution(12864420651747431604)
XLA Ops:
  0.6 0.0 copy-start
  0.6 0.9 %copy-done = bf16[384,96]{0,1:T(8,128)(2,1)S(1)} copy-done((bf16[384,96]{0,1:T(8,128)(2,1)S(1)}, bf16[384,96]{0,1:T(8,128)(2,1)}, u32[]{:S(2)}) %copy-start) | copy-done | bytes 73752
  1.5 0.0 copy-start.1
  1.5 0.0 copy-start.2
  1.5 79.2 %shard_map.100 = (bf16[96,128]{1,0:T(8,128)(2,1)S(1)}, bf16[96,128]{1,0:T(8,128)(2,1)S(1)}, f32[96,384]{1,0:T(8,128)S(1)}, bf16[96,384]{1,0:T(8,128)(2,1)S(1)}) custom-call(bf16[128,3072]{1,0:T(8,128)(2,1)} %inputs.1, bf16[128,3072]{1,0:T(8,128)(2,1)} %cotangent.1, bf16[96,384]{1,0:T(8,128)(2,1)S(1)} %bitcast.13, f32[96,384]{1,0:T(8,128)} %bitcast.17, ...), custom_call_target="tpu_custom_call" | custom-call | tf_op jit(solution)/shard_map/pallas_call | solution.py:664
  80.7 0.0 copy-done.1
  80.7 0.0 copy-done.2
  80.7 0.8 fusion.2
  81.5 0.6 copy.14
  82.1 0.6 copy.15
  82.8 0.6 copy.16
Async XLA Ops:
  0.6 0.9 %copy-start = (bf16[384,96]{0,1:T(8,128)(2,1)S(1)}, bf16[384,96]{0,1:T(8,128)(2,1)}, u32[]{:S(2)}) copy-start(bf16[384,96]{0,1:T(8,128)(2,1)} %param.7) | copy-start | bytes 221188
  1.5 79.2 %copy-start.1 = (f32[384,96]{0,1:T(8,128)S(1)}, f32[384,96]{0,1:T(8,128)}, u32[]{:S(2)}) copy-start(f32[384,96]{0,1:T(8,128)} %param.8) | copy-start | bytes 442372
  1.5 79.2 %copy-start.2 = (f32[384,96]{0,1:T(8,128)S(1)}, f32[384,96]{0,1:T(8,128)}, u32[]{:S(2)}) copy-start(f32[384,96]{0,1:T(8,128)} %param.9) | copy-start | bytes 442372
